TPU v7x, 32 devices: a whole 2x2x4 slice. The times are simulated.
32 devices in a mesh: proj: 8 (over z, y), grp: 4 (over x, core).
Axes of the slice: x: 2, y: 2, z: 4, core: 2. Of those that a mesh axis runs over, the one named last changes fastest.
Arguments:
- grads: bfloat16 [1024, 16384], P('grp', 'proj'), may hold values from -6 to 6
- proj_matrix: bfloat16 [16384, 8192], P('proj', 'grp'), may hold values from -48 to 48
- targets: bfloat16 [2048, 8192], P('proj', 'grp'), may hold values from -480 to 480
Outputs:
- scores: float32 [1024, 2048], P('proj', 'grp')
All inputs are finite; a program needn't handle non-finite values.
Results may differ from a plain program's by a relative error of at most 0.0029.
Values may be sent and summed in bfloat16 or wider, within the bound.
No kernel may reach another device: no remote copies, remote signals or barrier semaphores. Data moves between devices by JAX's collectives and lax.ppermute only.
A program may use at most 128 MiB of HBM per device.

v0:
```python
import jax
import jax.numpy as jnp
from jax import lax
from jax.sharding import PartitionSpec as P

K = 8192


def inner_rows(left, right):
    return lax.dot_general(
        left, right, (((1,), (1,)), ((), ())), preferred_element_type=jnp.float32
    )


def per_device(grads, proj_matrix, targets):
    gathered = lax.all_gather(grads, "grp", axis=0, tiled=True)
    features = lax.psum_scatter(
        jnp.dot(gathered, proj_matrix, preferred_element_type=jnp.float32),
        "proj",
        scatter_dimension=0,
        tiled=True,
    )
    rounded = features.astype(jnp.bfloat16)
    feature_sq = jnp.sum(jnp.square(rounded.astype(jnp.float32)), axis=1)
    target_all = lax.all_gather(targets, "proj", axis=0, tiled=True)
    target_sq = jnp.sum(jnp.square(target_all.astype(jnp.float32)), axis=1)
    products = inner_rows(rounded, target_all)
    feature_sq, target_sq = lax.psum((feature_sq, target_sq), "grp")
    products = lax.psum_scatter(products, "grp", scatter_dimension=1, tiled=True)
    own_cols = products.shape[1]
    target_sq = lax.dynamic_slice_in_dim(target_sq, lax.axis_index("grp") * own_cols, own_cols, 0)
    factor = float(K) ** 0.5
    return (
        factor
        * products
        * lax.rsqrt(feature_sq + 1e-06)[:, None]
        * lax.rsqrt(target_sq + 1e-06)[None, :]
    )


def solution(mesh):
    placed = (P("grp", "proj"), P("proj", "grp"), P("proj", "grp"))
    return jax.shard_map(
        per_device, mesh=mesh, in_specs=placed, out_specs=P("proj", "grp"), check_vma=False
    )
```

profile of v0, /device:TPU:0, one launch (start us, length us, event | category | flops | bytes accessed | tf_op | source)
XLA Modules:
  0.0 364.2 jit_solution(13749999797799309350)
XLA Ops:
  6.5 0.0 all-gather.3.cloned.1.call-start
  6.5 0.7 all-gather.3.cloned.1.call-update
  7.3 0.0 all-gather.5.cloned.1.call-start
  7.3 0.7 all-gather.5.cloned.1.call-update
  8.0 0.0 reduce-scatter.3.cloned.1.call-start
  8.1 38.1 %all-gather.3.cloned.1.call-done = bf16[1024,2048]{1,0:T(8,128)(2,1)} async-done(((bf16[256,2048]{1,0:T(8,128)(2,1)}), bf16[1024,2048]{1,0:T(8,128)(2,1)}) %all-gather.3.cloned.1.call-update) | async-done | bytes 4194320 | tf_op jit(solution)/shard_map/all_gather | solution.py:16
  46.1 14.4 %fusion.2 = f32[1024,2048]{1,0:T(8,128)} fusion(bf16[1024,2048]{1,0:T(8,128)(2,1)} %all-gather.3.cloned.1.call-done, bf16[2048,2048]{1,0:T(8,128)(2,1)} %param.4), kind=kOutput, calls=%fused_computation.7 | convolution fusion | flops 8589934592 | bytes 20971520 | tf_op jit(solution)/shard_map/dot_general | solution.py:18
  60.5 0.0 reduce-scatter.3.cloned.1.call-update
  60.5 0.0 reduce-scatter.5.cloned.1.call-start
  60.6 112.6 %all-gather.5.cloned.1.call-done = bf16[2048,2048]{1,0:T(8,128)(2,1)} async-done(((bf16[256,2048]{1,0:T(8,128)(2,1)}), bf16[2048,2048]{1,0:T(8,128)(2,1)}) %all-gather.5.cloned.1.call-update) | async-done | bytes 8388624 | tf_op jit(solution)/shard_map/all_gather | solution.py:25
  173.2 150.8 %reduce-scatter.3.cloned.1.call-done = f32[128,2048]{1,0:T(8,128)} async-done(((f32[1024,2048]{1,0:T(8,128)}), f32[128,2048]{1,0:T(8,128)}) %reduce-scatter.3.cloned.1.call-update) | async-done | bytes 1048592 | tf_op jit(solution)/shard_map/reduce_scatter | solution.py:17
  324.1 0.0 copy-start
  324.1 7.7 %fusion = f32[128,2048]{1,0:T(8,128)} fusion(bf16[2048,2048]{1,0:T(8,128)(2,1)} %all-gather.5.cloned.1.call-done, f32[128,2048]{1,0:T(8,128)} %reduce-scatter.3.cloned.1.call-done), kind=kOutput, calls=%fused_computation.3 | convolution fusion | flops 1074003968 | bytes 10485760 | tf_op jit(solution)/shard_map/dot_general | solution.py:10
  331.8 0.0 reduce-scatter.5.cloned.1.call-update
  331.8 5.1 %multiply_reduce_fusion = f32[2048]{0:T(1024)S(1)} fusion(bf16[2048,2048]{1,0:T(8,128)(2,1)} %all-gather.5.cloned.1.call-done), kind=kLoop, calls=%fused_computation | loop fusion | flops 12580864 | bytes 8396800 | tf_op jit(solution)/shard_map/reduce_sum | solution.py:26
  336.9 0.0 copy-done
  336.9 0.2 multiply_reduce_fusion.1
  337.1 7.1 %all-reduce = (f32[2048]{0:T(1024)S(1)}, f32[128]{0:T(128)S(1)}) all-reduce(f32[2048]{0:T(1024)S(1)} %multiply_reduce_fusion, f32[128]{0:T(128)S(1)} %multiply_reduce_fusion.1), channel_id=1, replica_groups=mesh['proj'=8,'grp'=4] {'grp'}, use_global_device_ids=true, to_apply=%region_5.0 | all-reduce | flops 2176 | bytes 17408 | tf_op jit(solution)/shard_map/psum | solution.py:28
  344.2 0.1 add_rsqrt_fusion
  344.3 11.6 %reduce-scatter.5.cloned.1.call-done = f32[128,512]{1,0:T(8,128)} async-done(((f32[128,2048]{1,0:T(8,128)}), f32[128,512]{1,0:T(8,128)}) %reduce-scatter.5.cloned.1.call-update) | async-done | bytes 262160 | tf_op jit(solution)/shard_map/reduce_scatter | solution.py:29
  355.9 1.7 multiply_multiply_fusion
  (1 shorter events, 0.0 us)
Async XLA Ops:
  6.5 39.6 %all-gather.3.cloned.1.call-start = ((), (), s32[]{:S(2)}) async-start(), calls=%async_computation.2 | async-start | bytes 5242880 | tf_op jit(solution)/shard_map/all_gather | solution.py:16
  7.3 166.0 %all-gather.5.cloned.1.call-start = ((), (), s32[]{:S(2)}) async-start(), calls=%async_computation.4 | async-start | bytes 9437184 | tf_op jit(solution)/shard_map/all_gather | solution.py:25
  8.0 316.1 %reduce-scatter.3.cloned.1.call-start = ((), (), s32[]{:S(2)}) async-start(), calls=%async_computation.3 | async-start | bytes 9437184 | tf_op jit(solution)/shard_map/reduce_scatter | solution.py:17
  60.5 295.3 %reduce-scatter.5.cloned.1.call-start = ((), (), s32[]{:S(2)}) async-start(), calls=%async_computation.5 | async-start | bytes 1310720 | tf_op jit(solution)/shard_map/reduce_scatter | solution.py:29
  324.1 12.8 %copy-start = (f32[128,2048]{1,0:T(8,128)S(1)}, f32[128,2048]{1,0:T(8,128)}, u32[]{:S(2)}) copy-start(f32[128,2048]{1,0:T(8,128)} %reduce-scatter.3.cloned.1.call-done) | copy-start | bytes 3145732
Sparse Core Ops, SparseCore 0:
  8.9 37.1 all-gather.2
  48.3 124.9 all-gather.4
  176.9 147.1 reduce-scatter.2
  332.0 23.8 reduce-scatter.4
where the time goes:
time: 364 us
  waiting for transfers between devices  315 us (87%)
  matrix products  22.1 us (6%)
  between operations  13.1 us (4%)
  blocking collectives  7.13 us (2%)
  other arithmetic  7.06 us (2%)
    reduce_scatter x1, waiting for transfers between devices, per_device(): lax.psum_scatter(jnp.dot(gathered, proj_matrix, preferred_element_type=jn...  151 us
    all_gather x1, waiting for transfers between devices, per_device(): target_all = lax.all_gather(targets, 'proj', axis=0, tiled=True)  113 us
    all_gather x1, waiting for transfers between devices, per_device(): gathered = lax.all_gather(grads, 'grp', axis=0, tiled=True)  38.1 us
    dot_general x1, matrix products, per_device(): jnp.dot(gathered, proj_matrix, preferred_element_type=jnp.float32)  14.4 us
    reduce_scatter x1, waiting for transfers between devices, per_device(): lax.psum_scatter(products, 'grp', scatter_dimension=1, tiled=True)  11.6 us
    dot_general x1, matrix products, inner_rows(): lax.dot_general(left, right, (((1,), (1,)), ((), ())), preferred_element_...  7.73 us
  transfers between devices with their start and end apart: 4, of which 4 were waited for; matrix products, arithmetic and copies ran while one was open for 5% of the time, Pallas kernels for 0%

commit v1 on v0

v1 whole, which is shorter than its diff:
```python
import math

import jax
import jax.numpy as jnp
from jax import lax
from jax.sharding import PartitionSpec as P

F32, BF16, F16 = jnp.float32, jnp.bfloat16, jnp.float16
EPS = 1e-06


def swap(value, axis, size, bit):
    return lax.ppermute(value, axis, [(i, i ^ bit) for i in range(size)])


def inner_rows(left, right):
    return lax.dot_general(
        left, right, (((1,), (1,)), ((), ())), preferred_element_type=F32
    )


def pick(value, index, axis=0):
    return lax.dynamic_index_in_dim(value, index, axis, keepdims=False)


def per_device(n_p, n_g, grads, proj_matrix, targets):
    n_z = n_p // 2
    p, g = lax.axis_index("proj"), lax.axis_index("grp")
    py, pz = p % 2, p // 2
    rows, depth = grads.shape
    width = proj_matrix.shape[1]
    tgt_rows = targets.shape[0]
    examples = rows * n_g
    own = examples // n_p
    piece = width // n_z
    half = rows // 2

    def over_z(block_of, bit):
        return swap(block_of(pz ^ bit), "proj", n_p, 2 * bit)

    grads_1 = swap(grads, "grp", n_g, 1)
    grads_2 = swap(grads, "grp", n_g, 2)
    grads_3 = swap(grads_2, "grp", n_g, 1)
    chunks = [grads, grads_1, grads_2, grads_3]

    def target_piece(z):
        return lax.dynamic_slice_in_dim(targets, z * piece, piece, 1)

    tgt = [target_piece(pz)] + [over_z(target_piece, bit) for bit in range(1, n_z)]

    row_max = jnp.max(jnp.abs(grads), axis=1).astype(F32) * jnp.max(jnp.abs(proj_matrix)).astype(F32)
    tgt_sq = jnp.sum(jnp.square(targets.astype(F32)), axis=1)
    row_max = lax.dynamic_update_slice_in_dim(jnp.zeros((examples,), F32), row_max, g * rows, 0)
    tgt_sq = lax.dynamic_update_slice_in_dim(jnp.zeros((tgt_rows * n_p,), F32), tgt_sq, p * tgt_rows, 0)
    steps = [("grp", n_g, 1 << k) for k in range(int(math.log2(n_g)))]
    steps += [("proj", n_p, 1 << k) for k in range(int(math.log2(n_p)))]
    for step in steps:
        both = swap(jnp.concatenate([row_max, tgt_sq]), *step)
        row_max = jnp.maximum(row_max, both[:examples])
        tgt_sq = tgt_sq + both[examples:]
    bound = row_max * float(depth * n_p)
    scale = jnp.exp2(jnp.clip(15.0 - jnp.ceil(jnp.log2(jnp.maximum(bound, 1e-30))), -40.0, 60.0))
    tgt_norm = lax.rsqrt(tgt_sq + EPS)

    def side(value, y):
        shape = (rows // (2 * own), 2, own) + value.shape[1:]
        return pick(value.reshape(shape), y, 1).reshape((half,) + value.shape[1:])

    def features_of(i, chunk):
        rows_scale = lax.dynamic_slice_in_dim(scale, (g ^ i) * rows, rows, 0)
        keep_scale = side(rows_scale, py)[:, None]
        part = jnp.dot(side(chunk, 1 - py), proj_matrix, preferred_element_type=F32)
        if i < 2:
            got = swap(part.astype(BF16), "proj", n_p, 1).astype(F32)
        else:
            send_scale = side(rows_scale, 1 - py)[:, None]
            got = swap((part * send_scale).astype(F16), "proj", n_p, 1).astype(F32)
        part = jnp.dot(side(chunk, py), proj_matrix, preferred_element_type=F32)
        part = (part + got) * keep_scale if i < 2 else part * keep_scale + got

        def block_of(z):
            return lax.dynamic_slice_in_dim(part, z * piece, piece, 1)

        total = block_of(pz)
        for bit in range(1, n_z):
            total = total + over_z(lambda z: block_of(z).astype(F16), bit).astype(F32)
        return total.astype(BF16)

    features = [features_of(i, chunk) for i, chunk in enumerate(chunks)]
    features = jnp.stack(features)
    features = jnp.concatenate([pick(features, b ^ g) for b in range(n_g)])
    feature_sq = jnp.sum(jnp.square(features.astype(F32)), axis=1)

    tgt = jnp.stack(tgt)
    other = swap(tgt, "proj", n_p, 1)
    pair = [jnp.where(py == 0, tgt, other), jnp.where(py == 0, other, tgt)]
    tgt = jnp.stack(pair, axis=1)
    tgt = jnp.stack([pick(tgt, pz ^ b) for b in range(n_z)])
    tgt = tgt.reshape(n_g, tgt_rows * n_p // n_g, piece)
    tgt_norm = tgt_norm.reshape(n_g, -1)

    def products_of(q):
        return inner_rows(features, pick(tgt, g ^ q))

    own_part = products_of(0) + swap(products_of(1), "grp", n_g, 1)
    far_part = products_of(2) + swap(products_of(3), "grp", n_g, 1)
    norm = [pick(tgt_norm, g ^ q)[None, :] / 64.0 for q in (0, 2)]
    part = own_part * norm[0] + swap((far_part * norm[1]).astype(F16), "grp", n_g, 2).astype(F32)

    part = part.reshape(n_z, own, -1)
    total = pick(part, pz)
    for bit in range(1, n_z):
        total = total + over_z(lambda z: pick(part, z).astype(F16), bit).astype(F32)

    for k in range(2):
        feature_sq = feature_sq + swap(feature_sq, "grp", n_g, 1 << k)
    for k in range(1, int(math.log2(n_p))):
        feature_sq = feature_sq + swap(feature_sq, "proj", n_p, 1 << k)
    feature_sq = pick(feature_sq.reshape(n_z, own), pz)
    own_scale = lax.dynamic_slice_in_dim(scale, p * own, own, 0)
    factor = 64.0 * float(width * n_g) ** 0.5
    return factor * total * lax.rsqrt(feature_sq + EPS * own_scale * own_scale)[:, None]


def solution(mesh):
    n_p, n_g = mesh.shape["proj"], mesh.shape["grp"]

    def body(grads, proj_matrix, targets):
        return per_device(n_p, n_g, grads, proj_matrix, targets)

    placed = (P("grp", "proj"), P("proj", "grp"), P("proj", "grp"))
    return jax.shard_map(
        body, mesh=mesh, in_specs=placed, out_specs=P("proj", "grp"), check_vma=False
    )
```

time: 364 us -> 176 us (0.48)
  waiting for transfers between devices: 315 us -> 75.5 us
  starting transfers between devices: 0.12 us -> 60.4 us
  between operations: 13.1 us -> 1.01 us
  blocking collectives: 7.13 us -> 0 us
  matrix products: 22.1 us -> 27.6 us
    reduce_scatter x2 -> x0, waiting for transfers between devices: 162 us -> none  [the longest x1 151 us: per_device(): lax.psum_scatter(jnp.dot(gathered, proj_matrix, preferred_element_type=jn...]
    all_gather x2 -> x0, waiting for transfers between devices: 151 us -> none  [the longest x1 113 us: per_device(): target_all = lax.all_gather(targets, 'proj', axis=0, tiled=True)]
    ppermute x0 -> x38, waiting for transfers between devices: none -> 75.5 us  [swap(): return lax.ppermute(value, axis, [(i, i ^ bit) for i in range(size)])]
    ppermute x0 -> x38, starting transfers between devices: none -> 60.4 us  [swap(): return lax.ppermute(value, axis, [(i, i ^ bit) for i in range(size)])]
    psum x1 -> x0, blocking collectives: 7.13 us -> none  [per_device(): feature_sq, target_sq = lax.psum((feature_sq, target_sq), 'grp')]
    reduce_max x0 -> x2, other arithmetic: none -> 6.32 us  [the longest x1 6.05 us: per_device(): jnp.max(jnp.abs(proj_matrix)).astype(F32)]
    dot_general x1 -> x8, matrix products: 14.4 us -> 20.5 us  [the longest x4 10.5 us: features_of(): part = jnp.dot(side(chunk, 1 - py), proj_matrix, preferred_element_type=F32)]
    reduce_sum x2, other arithmetic: 5.23 us -> 0.46 us  [the longest x1 0.29 us: per_device(): tgt_sq = jnp.sum(jnp.square(targets.astype(F32)), axis=1)]
  transfers between devices with their start and end apart: 4 -> 38, of which waited for: 4 -> 19; matrix products, arithmetic and copies ran while one was open for 5% -> 16% of each run, Pallas kernels for 0% -> 0%
where the time goes in v1:
time: 176 us; the launch traced here: 175 us
  waiting for transfers between devices  75.5 us (43%)
  starting transfers between devices  60.4 us (34%)
  matrix products  27.6 us (16%)
  other arithmetic  9.56 us (5%)
    ppermute x38, waiting for transfers between devices, swap(): return lax.ppermute(value, axis, [(i, i ^ bit) for i in range(size)])  75.5 us
    ppermute x38, starting transfers between devices, swap(): return lax.ppermute(value, axis, [(i, i ^ bit) for i in range(size)])  60.4 us
    dot_general x4, matrix products, features_of(): part = jnp.dot(side(chunk, 1 - py), proj_matrix, preferred_element_type=F32)  10.5 us
    dot_general x4, matrix products, features_of(): part = jnp.dot(side(chunk, py), proj_matrix, preferred_element_type=F32)  10.1 us
    dot_general x4, matrix products, inner_rows(): lax.dot_general(left, right, (((1,), (1,)), ((), ())), preferred_element_...  7.09 us
    reduce_max x1, other arithmetic, per_device(): jnp.max(jnp.abs(proj_matrix)).astype(F32)  6.05 us
  transfers between devices with their start and end apart: 38, of which 19 were waited for; matrix products, arithmetic and copies ran while one was open for 16% of the time, Pallas kernels for 0%

profile of v1, /device:TPU:0, one launch (start us, length us, event | category | flops | bytes accessed | tf_op | source)
XLA Modules:
  0.0 175.5 jit_solution(17492534387763246670)
XLA Ops:
  0.0 6.0 %abs_reduce_fusion = bf16[]{:T(256)} fusion(bf16[2048,2048]{1,0:T(8,128)(2,1)} %param.4), kind=kLoop, calls=%fused_computation | loop fusion | flops 8388607 | bytes 8388610 | tf_op jit(solution)/shard_map/reduce_max | solution.py:51
  9.3 2.9 %collective-permute-start.2 = (f32[3072]{0:T(1024)S(1)}, f32[3072]{0:T(1024)S(1)}, u32[]{:S(2)}, u32[]{:S(2)}) collective-permute-start(f32[3072]{0:T(1024)S(1)} %pad_maximum_fusion.5), channel_id=1, source_target_pairs={{0,2},{1,3},{2,0},{3,1},{4,6},{5,7},{6,4},{7,5},{8,10},{9,11},{10,... | collective-permute-start | bytes 36872 | tf_op jit(solution)/shard_map/ppermute | solution.py:13
  19.8 5.4 %convolution_convert_fusion.1 = bf16[128,2048]{1,0:T(8,128)(2,1)} fusion(bf16[2048,2048]{1,0:T(8,128)(2,1)} %param.4, bf16[1,2,128,2048]{3,2,1,0:T(8,128)(2,1)S(1)} %bitcast.125, s32[]{:T(128)S(6)} %select_n.133), kind=kOutput, calls=%fused_computation.18 | convolution fusion | flops 1074003968 | bytes 9437188 | tf_op jit(solution)/shard_map/dot_general | solution.py:72
  26.8 2.6 %collective-permute-start.5 = (f32[3072]{0:T(1024)S(1)}, f32[3072]{0:T(1024)S(1)}, u32[]{:S(2)}, u32[]{:S(2)}) collective-permute-start(f32[3072]{0:T(1024)S(1)} %pad_maximum_fusion.8), channel_id=1, source_target_pairs={{0,16},{4,20},{8,24},{12,28},{16,0},{20,4},{24,8},{28,12},{1,17},{... | collective-permute-start | bytes 36872 | tf_op jit(solution)/shard_map/ppermute | solution.py:13
  31.6 2.6 %collective-permute-start.25 = (bf16[256,512]{1,0:T(8,128)(2,1)}, bf16[256,512]{1,0:T(8,128)(2,1)S(1)}, u32[]{:S(2)}, u32[]{:S(2)}) collective-permute-start(bf16[256,512]{1,0:T(8,128)(2,1)} %get-tuple-element.29), channel_id=1, source_target_pairs={{0,16},{4,20},{8,24},{12,28},{16,0},{20,4},{24,8},{28,12},{1,17},{... | collective-permute-start | bytes 786440 | tf_op jit(solution)/shard_map/ppermute | solution.py:13
  34.3 4.3 %collective-permute-done = bf16[128,2048]{1,0:T(8,128)(2,1)} collective-permute-done((bf16[128,2048]{1,0:T(8,128)(2,1)}, bf16[128,2048]{1,0:T(8,128)(2,1)}, u32[]{:S(2)}, u32[]{:S(2)}) %collective-permute-start) | collective-permute-done | bytes 524320 | tf_op jit(solution)/shard_map/ppermute | solution.py:13
  38.7 2.4 %collective-permute-start.26 = (bf16[256,512]{1,0:T(8,128)(2,1)}, bf16[256,512]{1,0:T(8,128)(2,1)S(1)}, u32[]{:S(2)}, u32[]{:S(2)}) collective-permute-start(bf16[256,512]{1,0:T(8,128)(2,1)} %get-tuple-element.28), channel_id=1, source_target_pairs={{0,24},{4,28},{8,16},{12,20},{16,8},{20,12},{24,0},{28,4},{1,25},{... | collective-permute-start | bytes 786440 | tf_op jit(solution)/shard_map/ppermute | solution.py:13
  41.1 4.7 %add_multiply_fusion = f32[128,2048]{1,0:T(8,128)S(1)} fusion(bf16[128,2048]{1,0:T(8,128)(2,1)} %collective-permute-done, bf16[2048,2048]{1,0:T(8,128)(2,1)} %param.4, f32[128]{0:T(128)S(1)} %fusion.78, bf16[1,2,128,2048]{3,2,1,0:T(8,128)(2,1)S(1)} %bitcast.126, s32[]{:T(128)S(6)} %select_n.132), kind=kOutput, calls=%fused_computation.34 | convolution fusion | flops 1074528256 | bytes 10486276 | tf_op jit(solution)/shard_map/dot_general | solution.py:78
  46.6 5.0 %collective-permute-done.25 = bf16[256,512]{1,0:T(8,128)(2,1)S(1)} collective-permute-done((bf16[256,512]{1,0:T(8,128)(2,1)}, bf16[256,512]{1,0:T(8,128)(2,1)S(1)}, u32[]{:S(2)}, u32[]{:S(2)}) %collective-permute-start.25) | collective-permute-done | bytes 262176 | tf_op jit(solution)/shard_map/ppermute | solution.py:13
  51.6 2.9 %collective-permute-start.8 = (f16[128,512]{1,0:T(8,128)(2,1)S(1)}, f16[128,512]{1,0:T(8,128)(2,1)S(1)}, u32[]{:S(2)}, u32[]{:S(2)}) collective-permute-start(f16[128,512]{1,0:T(8,128)(2,1)S(1)} %get-tuple-element.15), channel_id=1, source_target_pairs={{0,24},{4,28},{8,16},{12,20},{16,8},{20,12},{24,0},{28,4},{1,25},{... | collective-permute-start | bytes 393224 | tf_op jit(solution)/shard_map/ppermute | solution.py:13
  55.9 8.1 %collective-permute-done.7 = f16[128,512]{1,0:T(8,128)(2,1)S(1)} collective-permute-done((f16[128,512]{1,0:T(8,128)(2,1)S(1)}, f16[128,512]{1,0:T(8,128)(2,1)S(1)}, u32[]{:S(2)}, u32[]{:S(2)}) %collective-permute-start.7) | collective-permute-done | bytes 131104 | tf_op jit(solution)/shard_map/ppermute | solution.py:13
  70.1 10.8 %collective-permute-done.27 = bf16[4,256,512]{2,1,0:T(8,128)(2,1)S(1)} collective-permute-done((bf16[4,256,512]{2,1,0:T(8,128)(2,1)S(1)}, bf16[4,256,512]{2,1,0:T(8,128)(2,1)S(1)}, u32[]{:S(2)}, u32[]{:S(2)}) %collective-permute-start.27) | collective-permute-done | bytes 1048608 | tf_op jit(solution)/shard_map/ppermute | solution.py:13
  81.5 10.5 %collective-permute-done.10 = bf16[128,2048]{1,0:T(8,128)(2,1)S(1)} collective-permute-done((bf16[128,2048]{1,0:T(8,128)(2,1)S(1)}, bf16[128,2048]{1,0:T(8,128)(2,1)S(1)}, u32[]{:S(2)}, u32[]{:S(2)}) %collective-permute-start.10) | collective-permute-done | bytes 524320 | tf_op jit(solution)/shard_map/ppermute | solution.py:13
  94.5 9.1 %collective-permute-start.11 = (f16[128,512]{1,0:T(8,128)(2,1)S(1)}, f16[128,512]{1,0:T(8,128)(2,1)S(1)}, u32[]{:S(2)}, u32[]{:S(2)}) collective-permute-start(f16[128,512]{1,0:T(8,128)(2,1)S(1)} %get-tuple-element.17), channel_id=1, source_target_pairs={{0,8},{4,12},{8,0},{12,4},{16,24},{20,28},{24,16},{28,20},{1,9},{5... | collective-permute-start | bytes 393224 | tf_op jit(solution)/shard_map/ppermute | solution.py:13
  103.7 2.4 %collective-permute-start.13 = (f16[128,512]{1,0:T(8,128)(2,1)S(1)}, f16[128,512]{1,0:T(8,128)(2,1)S(1)}, u32[]{:S(2)}, u32[]{:S(2)}) collective-permute-start(f16[128,512]{1,0:T(8,128)(2,1)S(1)} %get-tuple-element.18), channel_id=1, source_target_pairs={{0,24},{4,28},{8,16},{12,20},{16,8},{20,12},{24,0},{28,4},{1,25},{... | collective-permute-start | bytes 393224 | tf_op jit(solution)/shard_map/ppermute | solution.py:13
  110.2 3.6 %collective-permute-start.16 = (f16[128,512]{1,0:T(8,128)(2,1)S(1)}, f16[128,512]{1,0:T(8,128)(2,1)S(1)}, u32[]{:S(2)}, u32[]{:S(2)}) collective-permute-start(f16[128,512]{1,0:T(8,128)(2,1)S(1)} %get-tuple-element.20), channel_id=1, source_target_pairs={{0,8},{4,12},{8,0},{12,4},{16,24},{20,28},{24,16},{28,20},{1,9},{5... | collective-permute-start | bytes 393224 | tf_op jit(solution)/shard_map/ppermute | solution.py:13
  118.3 3.7 %collective-permute-start.21 = (f16[128,512]{1,0:T(8,128)(2,1)S(1)}, f16[128,512]{1,0:T(8,128)(2,1)S(1)}, u32[]{:S(2)}, u32[]{:S(2)}) collective-permute-start(f16[128,512]{1,0:T(8,128)(2,1)S(1)} %get-tuple-element.23), channel_id=1, source_target_pairs={{0,8},{4,12},{8,0},{12,4},{16,24},{20,28},{24,16},{28,20},{1,9},{5... | collective-permute-start | bytes 393224 | tf_op jit(solution)/shard_map/ppermute | solution.py:13
  122.1 2.4 %collective-permute-start.23 = (f16[128,512]{1,0:T(8,128)(2,1)S(1)}, f16[128,512]{1,0:T(8,128)(2,1)S(1)}, u32[]{:S(2)}, u32[]{:S(2)}) collective-permute-start(f16[128,512]{1,0:T(8,128)(2,1)S(1)} %get-tuple-element.24), channel_id=1, source_target_pairs={{0,24},{4,28},{8,16},{12,20},{16,8},{20,12},{24,0},{28,4},{1,25},{... | collective-permute-start | bytes 393224 | tf_op jit(solution)/shard_map/ppermute | solution.py:13
  124.5 5.0 %collective-permute-done.17 = f16[128,512]{1,0:T(8,128)(2,1)S(1)} collective-permute-done((f16[128,512]{1,0:T(8,128)(2,1)S(1)}, f16[128,512]{1,0:T(8,128)(2,1)S(1)}, u32[]{:S(2)}, u32[]{:S(2)}) %collective-permute-start.17) | collective-permute-done | bytes 131104 | tf_op jit(solution)/shard_map/ppermute | solution.py:13
  129.6 4.9 %collective-permute-done.22 = f16[128,512]{1,0:T(8,128)(2,1)S(1)} collective-permute-done((f16[128,512]{1,0:T(8,128)(2,1)S(1)}, f16[128,512]{1,0:T(8,128)(2,1)S(1)}, u32[]{:S(2)}, u32[]{:S(2)}) %collective-permute-start.22) | collective-permute-done | bytes 131104 | tf_op jit(solution)/shard_map/ppermute | solution.py:13
  139.1 2.5 %fusion.8 = f16[512,512]{1,0:T(8,128)(2,1)} fusion(f32[512,512]{1,0:T(8,128)} %collective-permute-done.29, f32[512]{0:T(512)S(1)} %bitcast.144, bf16[4,512,512]{2,1,0:T(8,128)(2,1)S(1)} %bitcast.129, s32[]{:T(128)S(6)} %select_n.146, bf16[128,512]{1,0:T(8,128)(2,1)S(1)} %get-tuple-element.31, bf16[128,512]{1,0:T(8,128)(2,1)S(1)} %get-tuple-element.32, ...), kind=kOutput, calls=%fused_computation.28 | convolution fusion | flops 271319040 | bytes 2623492 | tf_op jit(solution)/shard_map/dot_general | solution.py:17
  145.0 10.8 %collective-permute-done.35 = f32[512]{0:T(512)S(1)} collective-permute-done((f32[512]{0:T(512)S(1)}, f32[512]{0:T(512)S(1)}, u32[]{:S(2)}, u32[]{:S(2)}) %collective-permute-start.35) | collective-permute-done | bytes 2080 | tf_op jit(solution)/shard_map/ppermute | solution.py:13
  163.4 2.8 %collective-permute-start.32 = (f16[128,512]{1,0:T(8,128)(2,1)S(1)}, f16[128,512]{1,0:T(8,128)(2,1)S(1)}, u32[]{:S(2)}, u32[]{:S(2)}) collective-permute-start(f16[128,512]{1,0:T(8,128)(2,1)S(1)} %get-tuple-element.13), channel_id=1, source_target_pairs={{0,16},{4,20},{8,24},{12,28},{16,0},{20,4},{24,8},{28,12},{1,17},{... | collective-permute-start | bytes 393224 | tf_op jit(solution)/shard_map/ppermute | solution.py:13
  170.1 4.6 %collective-permute-done.32 = f16[128,512]{1,0:T(8,128)(2,1)S(1)} collective-permute-done((f16[128,512]{1,0:T(8,128)(2,1)S(1)}, f16[128,512]{1,0:T(8,128)(2,1)S(1)}, u32[]{:S(2)}, u32[]{:S(2)}) %collective-permute-start.32) | collective-permute-done | bytes 131104 | tf_op jit(solution)/shard_map/ppermute | solution.py:13
  (126 shorter events, 54.3 us)
Async XLA Ops:
  16.0 48.2 %collective-permute-start.9 = (bf16[256,2048]{1,0:T(8,128)(2,1)S(1)}, bf16[256,2048]{1,0:T(8,128)(2,1)}, u32[]{:S(2)}, u32[]{:S(2)}) collective-permute-start(bf16[256,2048]{1,0:T(8,128)(2,1)S(1)} %copy-done.1), channel_id=1, source_target_pairs={{0,1},{1,0},{2,3},{3,2},{4,5},{5,4},{6,7},{7,6},{8,9},{9,8},{10,11... | collective-permute-start | bytes 3145736 | tf_op jit(solution)/shard_map/ppermute | solution.py:13
  16.0 52.3 %collective-permute-start.14 = (bf16[256,2048]{1,0:T(8,128)(2,1)S(1)}, bf16[256,2048]{1,0:T(8,128)(2,1)S(1)}, u32[]{:S(2)}, u32[]{:S(2)}) collective-permute-start(bf16[256,2048]{1,0:T(8,128)(2,1)S(1)} %copy-done.1), channel_id=1, source_target_pairs={{0,2},{1,3},{2,0},{3,1},{4,6},{5,7},{6,4},{7,5},{8,10},{9,11},{10,... | collective-permute-start | bytes 3145736 | tf_op jit(solution)/shard_map/ppermute | solution.py:13
  25.2 13.4 %collective-permute-start = (bf16[128,2048]{1,0:T(8,128)(2,1)}, bf16[128,2048]{1,0:T(8,128)(2,1)}, u32[]{:S(2)}, u32[]{:S(2)}) collective-permute-start(bf16[128,2048]{1,0:T(8,128)(2,1)} %convolution_convert_fusion.1), channel_id=1, source_target_pairs={{0,4},{4,0},{8,12},{12,8},{16,20},{20,16},{24,28},{28,24},{1,5},{5... | collective-permute-start | bytes 1572872 | tf_op jit(solution)/shard_map/ppermute | solution.py:13
  30.3 15.6 %collective-permute-start.24 = (bf16[256,512]{1,0:T(8,128)(2,1)}, bf16[256,512]{1,0:T(8,128)(2,1)S(1)}, u32[]{:S(2)}, u32[]{:S(2)}) collective-permute-start(bf16[256,512]{1,0:T(8,128)(2,1)} %get-tuple-element.27), channel_id=1, source_target_pairs={{0,8},{4,12},{8,0},{12,4},{16,24},{20,28},{24,16},{28,20},{1,9},{5... | collective-permute-start | bytes 786440 | tf_op jit(solution)/shard_map/ppermute | solution.py:13
  31.6 20.0 %collective-permute-start.25 = (bf16[256,512]{1,0:T(8,128)(2,1)}, bf16[256,512]{1,0:T(8,128)(2,1)S(1)}, u32[]{:S(2)}, u32[]{:S(2)}) collective-permute-start(bf16[256,512]{1,0:T(8,128)(2,1)} %get-tuple-element.29), channel_id=1, source_target_pairs={{0,16},{4,20},{8,24},{12,28},{16,0},{20,4},{24,8},{28,12},{1,17},{... | collective-permute-start | bytes 786440 | tf_op jit(solution)/shard_map/ppermute | solution.py:13
  38.7 13.0 %collective-permute-start.26 = (bf16[256,512]{1,0:T(8,128)(2,1)}, bf16[256,512]{1,0:T(8,128)(2,1)S(1)}, u32[]{:S(2)}, u32[]{:S(2)}) collective-permute-start(bf16[256,512]{1,0:T(8,128)(2,1)} %get-tuple-element.28), channel_id=1, source_target_pairs={{0,24},{4,28},{8,16},{12,20},{16,8},{20,12},{24,0},{28,4},{1,25},{... | collective-permute-start | bytes 786440 | tf_op jit(solution)/shard_map/ppermute | solution.py:13
  51.6 12.4 %collective-permute-start.7 = (f16[128,512]{1,0:T(8,128)(2,1)S(1)}, f16[128,512]{1,0:T(8,128)(2,1)S(1)}, u32[]{:S(2)}, u32[]{:S(2)}) collective-permute-start(f16[128,512]{1,0:T(8,128)(2,1)S(1)} %get-tuple-element.16), channel_id=1, source_target_pairs={{0,16},{4,20},{8,24},{12,28},{16,0},{20,4},{24,8},{28,12},{1,17},{... | collective-permute-start | bytes 393224 | tf_op jit(solution)/shard_map/ppermute | solution.py:13
  51.6 12.4 %collective-permute-start.8 = (f16[128,512]{1,0:T(8,128)(2,1)S(1)}, f16[128,512]{1,0:T(8,128)(2,1)S(1)}, u32[]{:S(2)}, u32[]{:S(2)}) collective-permute-start(f16[128,512]{1,0:T(8,128)(2,1)S(1)} %get-tuple-element.15), channel_id=1, source_target_pairs={{0,24},{4,28},{8,16},{12,20},{16,8},{20,12},{24,0},{28,4},{1,25},{... | collective-permute-start | bytes 393224 | tf_op jit(solution)/shard_map/ppermute | solution.py:13
  54.7 26.2 %collective-permute-start.27 = (bf16[4,256,512]{2,1,0:T(8,128)(2,1)S(1)}, bf16[4,256,512]{2,1,0:T(8,128)(2,1)S(1)}, u32[]{:S(2)}, u32[]{:S(2)}) collective-permute-start(bf16[4,256,512]{2,1,0:T(8,128)(2,1)S(1)} %pad_maximum_fusion.1), channel_id=1, source_target_pairs={{0,4},{4,0},{8,12},{12,8},{16,20},{20,16},{24,28},{28,24},{1,5},{5... | collective-permute-start | bytes 3145736 | tf_op jit(solution)/shard_map/ppermute | solution.py:13
  66.6 25.5 %collective-permute-start.10 = (bf16[128,2048]{1,0:T(8,128)(2,1)S(1)}, bf16[128,2048]{1,0:T(8,128)(2,1)S(1)}, u32[]{:S(2)}, u32[]{:S(2)}) collective-permute-start(bf16[128,2048]{1,0:T(8,128)(2,1)S(1)} %convolution_convert_fusion), channel_id=1, source_target_pairs={{0,4},{4,0},{8,12},{12,8},{16,20},{20,16},{24,28},{28,24},{1,5},{5... | collective-permute-start | bytes 1572872 | tf_op jit(solution)/shard_map/ppermute | solution.py:13
  69.6 39.1 %collective-permute-start.15 = (f16[128,2048]{1,0:T(8,128)(2,1)S(1)}, f16[128,2048]{1,0:T(8,128)(2,1)S(1)}, u32[]{:S(2)}, u32[]{:S(2)}) collective-permute-start(f16[128,2048]{1,0:T(8,128)(2,1)S(1)} %fusion.3), channel_id=1, source_target_pairs={{0,4},{4,0},{8,12},{12,8},{16,20},{20,16},{24,28},{28,24},{1,5},{5... | collective-permute-start | bytes 1572872 | tf_op jit(solution)/shard_map/ppermute | solution.py:13
  70.1 36.0 %collective-permute-start.19 = (bf16[256,2048]{1,0:T(8,128)(2,1)S(1)}, bf16[256,2048]{1,0:T(8,128)(2,1)S(1)}, u32[]{:S(2)}, u32[]{:S(2)}) collective-permute-start(bf16[256,2048]{1,0:T(8,128)(2,1)S(1)} %collective-permute-done.14), channel_id=1, source_target_pairs={{0,1},{1,0},{2,3},{3,2},{4,5},{5,4},{6,7},{7,6},{8,9},{9,8},{10,11... | collective-permute-start | bytes 3145736 | tf_op jit(solution)/shard_map/ppermute | solution.py:13
  94.5 19.3 %collective-permute-start.11 = (f16[128,512]{1,0:T(8,128)(2,1)S(1)}, f16[128,512]{1,0:T(8,128)(2,1)S(1)}, u32[]{:S(2)}, u32[]{:S(2)}) collective-permute-start(f16[128,512]{1,0:T(8,128)(2,1)S(1)} %get-tuple-element.17), channel_id=1, source_target_pairs={{0,8},{4,12},{8,0},{12,4},{16,24},{20,28},{24,16},{28,20},{1,9},{5... | collective-permute-start | bytes 393224 | tf_op jit(solution)/shard_map/ppermute | solution.py:13
  103.7 11.8 %collective-permute-start.12 = (f16[128,512]{1,0:T(8,128)(2,1)S(1)}, f16[128,512]{1,0:T(8,128)(2,1)S(1)}, u32[]{:S(2)}, u32[]{:S(2)}) collective-permute-start(f16[128,512]{1,0:T(8,128)(2,1)S(1)} %get-tuple-element.19), channel_id=1, source_target_pairs={{0,16},{4,20},{8,24},{12,28},{16,0},{20,4},{24,8},{28,12},{1,17},{... | collective-permute-start | bytes 393224 | tf_op jit(solution)/shard_map/ppermute | solution.py:13
  103.7 12.7 %collective-permute-start.13 = (f16[128,512]{1,0:T(8,128)(2,1)S(1)}, f16[128,512]{1,0:T(8,128)(2,1)S(1)}, u32[]{:S(2)}, u32[]{:S(2)}) collective-permute-start(f16[128,512]{1,0:T(8,128)(2,1)S(1)} %get-tuple-element.18), channel_id=1, source_target_pairs={{0,24},{4,28},{8,16},{12,20},{16,8},{20,12},{24,0},{28,4},{1,25},{... | collective-permute-start | bytes 393224 | tf_op jit(solution)/shard_map/ppermute | solution.py:13
  110.2 11.8 %collective-permute-start.16 = (f16[128,512]{1,0:T(8,128)(2,1)S(1)}, f16[128,512]{1,0:T(8,128)(2,1)S(1)}, u32[]{:S(2)}, u32[]{:S(2)}) collective-permute-start(f16[128,512]{1,0:T(8,128)(2,1)S(1)} %get-tuple-element.20), channel_id=1, source_target_pairs={{0,8},{4,12},{8,0},{12,4},{16,24},{20,28},{24,16},{28,20},{1,9},{5... | collective-permute-start | bytes 393224 | tf_op jit(solution)/shard_map/ppermute | solution.py:13
  113.9 15.6 %collective-permute-start.17 = (f16[128,512]{1,0:T(8,128)(2,1)S(1)}, f16[128,512]{1,0:T(8,128)(2,1)S(1)}, u32[]{:S(2)}, u32[]{:S(2)}) collective-permute-start(f16[128,512]{1,0:T(8,128)(2,1)S(1)} %get-tuple-element.22), channel_id=1, source_target_pairs={{0,16},{4,20},{8,24},{12,28},{16,0},{20,4},{24,8},{28,12},{1,17},{... | collective-permute-start | bytes 393224 | tf_op jit(solution)/shard_map/ppermute | solution.py:13
  115.5 14.0 %collective-permute-start.18 = (f16[128,512]{1,0:T(8,128)(2,1)S(1)}, f16[128,512]{1,0:T(8,128)(2,1)S(1)}, u32[]{:S(2)}, u32[]{:S(2)}) collective-permute-start(f16[128,512]{1,0:T(8,128)(2,1)S(1)} %get-tuple-element.21), channel_id=1, source_target_pairs={{0,24},{4,28},{8,16},{12,20},{16,8},{20,12},{24,0},{28,4},{1,25},{... | collective-permute-start | bytes 393224 | tf_op jit(solution)/shard_map/ppermute | solution.py:13
  122.1 12.4 %collective-permute-start.22 = (f16[128,512]{1,0:T(8,128)(2,1)S(1)}, f16[128,512]{1,0:T(8,128)(2,1)S(1)}, u32[]{:S(2)}, u32[]{:S(2)}) collective-permute-start(f16[128,512]{1,0:T(8,128)(2,1)S(1)} %get-tuple-element.25), channel_id=1, source_target_pairs={{0,16},{4,20},{8,24},{12,28},{16,0},{20,4},{24,8},{28,12},{1,17},{... | collective-permute-start | bytes 393224 | tf_op jit(solution)/shard_map/ppermute | solution.py:13
  122.1 12.4 %collective-permute-start.23 = (f16[128,512]{1,0:T(8,128)(2,1)S(1)}, f16[128,512]{1,0:T(8,128)(2,1)S(1)}, u32[]{:S(2)}, u32[]{:S(2)}) collective-permute-start(f16[128,512]{1,0:T(8,128)(2,1)S(1)} %get-tuple-element.24), channel_id=1, source_target_pairs={{0,24},{4,28},{8,16},{12,20},{16,8},{20,12},{24,0},{28,4},{1,25},{... | collective-permute-start | bytes 393224 | tf_op jit(solution)/shard_map/ppermute | solution.py:13
  137.6 23.9 %collective-permute-start.28 = (f32[512,512]{1,0:T(8,128)}, f32[512,512]{1,0:T(8,128)}, u32[]{:S(2)}, u32[]{:S(2)}) collective-permute-start(f32[512,512]{1,0:T(8,128)} %fusion.16), channel_id=1, source_target_pairs={{0,1},{1,0},{2,3},{3,2},{4,5},{5,4},{6,7},{7,6},{8,9},{9,8},{10,11... | collective-permute-start | bytes 3145736 | tf_op jit(solution)/shard_map/ppermute | solution.py:13
  141.6 19.9 %collective-permute-start.30 = (f16[512,512]{1,0:T(8,128)(2,1)}, f16[512,512]{1,0:T(8,128)(2,1)S(1)}, u32[]{:S(2)}, u32[]{:S(2)}) collective-permute-start(f16[512,512]{1,0:T(8,128)(2,1)} %fusion.8), channel_id=1, source_target_pairs={{0,2},{1,3},{2,0},{3,1},{4,6},{5,7},{6,4},{7,5},{8,10},{9,11},{10,... | collective-permute-start | bytes 1572872 | tf_op jit(solution)/shard_map/ppermute | solution.py:13
  144.3 11.5 %collective-permute-start.35 = (f32[512]{0:T(512)S(1)}, f32[512]{0:T(512)S(1)}, u32[]{:S(2)}, u32[]{:S(2)}) collective-permute-start(f32[512]{0:T(512)S(1)} %add.266), channel_id=1, source_target_pairs={{0,2},{1,3},{2,0},{3,1},{4,6},{5,7},{6,4},{7,5},{8,10},{9,11},{10,... | collective-permute-start | bytes 6152 | tf_op jit(solution)/shard_map/ppermute | solution.py:13
  163.4 11.3 %collective-permute-start.32 = (f16[128,512]{1,0:T(8,128)(2,1)S(1)}, f16[128,512]{1,0:T(8,128)(2,1)S(1)}, u32[]{:S(2)}, u32[]{:S(2)}) collective-permute-start(f16[128,512]{1,0:T(8,128)(2,1)S(1)} %get-tuple-element.13), channel_id=1, source_target_pairs={{0,16},{4,20},{8,24},{12,28},{16,0},{20,4},{24,8},{28,12},{1,17},{... | collective-permute-start | bytes 393224 | tf_op jit(solution)/shard_map/ppermute | solution.py:13
  (18 other events, 148.9 us)

commit v2 on v0

v2 whole, which is shorter than its diff:
```python
import math

import jax
import jax.numpy as jnp
from jax import lax
from jax.sharding import PartitionSpec as P

F32, BF16, F16 = jnp.float32, jnp.bfloat16, jnp.float16
EPS = 1e-06


def swap(value, axis, size, bit):
    return lax.ppermute(value, axis, [(i, i ^ bit) for i in range(size)])


def inner_rows(left, right):
    return lax.dot_general(
        left, right, (((1,), (1,)), ((), ())), preferred_element_type=F32
    )


def pick(value, index, axis=0):
    return lax.dynamic_index_in_dim(value, index, axis, keepdims=False)


def after(value, earlier):
    cols, width = value.shape[-1], earlier.shape[-1]
    row = earlier[(0,) * (earlier.ndim - 1)]
    row = jnp.tile(row, cols // width) if cols > width else row[:cols]
    return value + (0.0 * row.astype(F32)).astype(value.dtype)


def encode(value, gain):
    return (value * (lax.rsqrt(jnp.maximum(jnp.abs(value), 1e-35)) * gain)).astype(F16)


def decode(code, gain):
    code = code.astype(F32)
    return code * jnp.abs(code) * (1.0 / (gain * gain))


MOST_GRAD, MOST_PROJ, MOST_TARGET = 16.0, 48.0, 480.0
NORM_GAIN = 0.5


def gain_for(most):
    return 2.0 ** math.floor(15.99 - 0.5 * math.log2(most))


def per_device(n_p, n_g, grads, proj_matrix, targets):
    n_z = n_p // 2
    p, g = lax.axis_index("proj"), lax.axis_index("grp")
    py, pz = p % 2, p // 2
    rows = grads.shape[0]
    width = proj_matrix.shape[1]
    tgt_rows = targets.shape[0]
    own = rows * n_g // n_p
    piece = width // n_z
    half = rows // 2

    most_feature = grads.shape[1] * n_p * MOST_GRAD * MOST_PROJ
    feature_gain = gain_for(most_feature)
    product_gain = gain_for(most_feature * MOST_TARGET * piece * n_g)

    z_bits = [1 << k for k in range(n_z.bit_length() - 1)]

    def reversed_bits(z):
        return sum(((z >> k) & 1) << (len(z_bits) - 1 - k) for k in range(len(z_bits)))

    last, flags = [None], {"gate": True, "mark": True}

    def then(value):
        return value if last[0] is None or not flags["gate"] else after(value, last[0])

    def done(value):
        if flags["mark"]:
            last[0] = value
        return value

    def step(work, *args, gate=True, mark=True):
        flags.update(gate=gate, mark=mark)
        return work(*args)

    def side(value, y):
        shape = (rows // (2 * own), 2, own) + value.shape[1:]
        return pick(value.reshape(shape), y, 1).reshape((half,) + value.shape[1:])

    order = sorted(range(n_z), key=lambda k: [k & bit for bit in z_bits])


    def columns(value):
        return jnp.stack([lax.dynamic_slice_in_dim(value, (pz ^ k) * piece, piece, 1) for k in order])

    kept, code, features = {}, {}, {}

    def partial(i, chunk):
        part = done(jnp.dot(then(chunk), proj_matrix, preferred_element_type=F32))
        kept[i] = side(part, py)
        code[i] = swap(encode(side(part, 1 - py), feature_gain), "proj", n_p, 1)

    def partial_away(i, chunk):
        part = done(jnp.dot(then(side(chunk, 1 - py)), proj_matrix, preferred_element_type=F32))
        code[i] = swap(encode(part, feature_gain), "proj", n_p, 1)

    def partial_kept(i, chunk):
        kept[i] = done(jnp.dot(then(side(chunk, py)), proj_matrix, preferred_element_type=F32))

    def collect(i):
        return done(then(kept[i]) + decode(code[i], feature_gain))

    def spread(i, bit):
        part = collect(i)
        part = columns(part) if bit == 1 else part
        kept[i], away = jnp.split(part, 2)
        code[i] = swap(encode(away, feature_gain), "proj", n_p, 2 * bit)

    def finish(i):
        features[i] = collect(i)[0].astype(BF16)

    def targets_over_z(blocks, bit):
        blocks = then(blocks)
        low, high = jnp.split(blocks, 2, axis=2)
        upper = (pz // bit) % 2 == 1
        return jnp.where(upper, high, low), swap(jnp.where(upper, low, high), "proj", n_p, 2 * bit)

    def joined(keep, got):
        return done(jnp.concatenate([keep, then(got)]))

    grads_2 = swap(grads, "grp", n_g, 2)
    grads_1 = swap(grads, "grp", n_g, 1)

    step(partial, 0, grads)
    grads_3 = swap(grads_2, "grp", n_g, 1)
    tgt = step(targets_over_z, targets[None], z_bits[-1])
    step(partial, 1, grads_1)
    step(spread, 0, 1)
    step(partial_away, 2, grads_2)
    step(spread, 1, 1)
    step(partial_kept, 2, grads_2)
    for bit in z_bits[-2::-1]:
        tgt = step(targets_over_z, step(joined, *tgt), bit, gate=False)
    step(partial_away, 3, grads_3)
    step(partial_kept, 3, grads_3)
    step(spread, 2, 1)
    for bit in z_bits[1:]:
        step(spread, 0, bit, mark=False)
    tgt = step(joined, *tgt)
    other = swap(tgt, "proj", n_p, 1)
    for bit in z_bits[1:]:
        step(spread, 1, bit)
    step(finish, 0)
    step(spread, 3, 1, gate=False)
    for bit in z_bits[1:]:
        step(spread, 2, bit, gate=False)
    step(finish, 1)
    for bit in z_bits[1:]:
        step(spread, 3, bit)
    step(finish, 2)
    step(finish, 3)

    in_chunk = n_z // n_g

    def row_block(z):
        return pick(features, ((z // in_chunk) ^ g) * in_chunk + z % in_chunk)

    features = jnp.stack([features[i] for i in range(n_g)]).reshape(n_z, own, piece)
    features = jnp.stack([row_block(pz ^ k) for k in range(n_z)])
    feature_sq = jnp.sum(jnp.square(features.astype(F32)), axis=2)
    features = features.reshape(n_z * own, piece)

    def of_member(q, mine, partners):
        places = [reversed_bits(pz ^ ((g ^ q) * in_chunk + n)) for n in range(in_chunk)]
        return jnp.concatenate([pick(value, at) for at in places for value in (mine, partners)])

    def products_of(q):
        return inner_rows(features, of_member(q, tgt, other)).reshape(n_z, own, -1)

    far, near = slice(1, n_z), slice(0, 1)
    prods = {3: products_of(3)}
    got_3 = swap(done(prods[3]), "grp", n_g, 1)
    prods[2] = products_of(2)
    prods[1] = products_of(1)
    got_1 = swap(then(prods[1]), "grp", n_g, 1)
    prods[0] = products_of(0)
    far_part = prods[2] + got_3
    own_part = prods[0] + got_1

    tgt_sq = [jnp.sum(jnp.square(value.astype(F32)), axis=2) for value in (tgt, other)]
    tgt_sq = jnp.stack([of_member(q, *tgt_sq) for q in range(n_g)])
    cols = tgt_sq.shape[1]
    got = swap(jnp.concatenate([feature_sq.reshape(-1), tgt_sq[1], tgt_sq[3]]), "grp", n_g, 1)
    feature_sq = feature_sq + got[: n_z * own].reshape(n_z, own)
    tgt_sq = [tgt_sq[2 * n] + got[n_z * own + n * cols :][:cols] for n in range(2)]

    def norm_rows(feature_sq, tgt_sq):
        rows = jnp.concatenate([jnp.pad(feature_sq, ((0, 0), (0, cols - own))), tgt_sq[None]])
        return jnp.pad(rows, ((0, -rows.shape[0] % 16), (0, 0)))

    def coded(product, norms):
        return jnp.concatenate([encode(product, product_gain), encode(jnp.sqrt(norms), NORM_GAIN)])

    def decoded(code, rows):
        product, norms = jnp.split(code, [rows])
        return decode(product, product_gain), jnp.square(decode(norms, NORM_GAIN))

    far_rows = (n_z - 1) * own
    codes = [swap(coded(far_part[far].reshape(far_rows, cols), norm_rows(feature_sq, tgt_sq[1])), "grp", n_g, 2)]
    codes.append(swap(encode(far_part[near][0], product_gain), "grp", n_g, 2))
    got, got_norms = decoded(codes[0], far_rows)
    part = done(then(own_part[far]) + got.reshape(n_z - 1, own, cols))
    feature_sq = feature_sq + got_norms[:n_z, :own]
    tgt_sq = tgt_sq[0] + got_norms[n_z]

    norms = [norm_rows(feature_sq[k : k + 1], tgt_sq) for k in range(n_z)]
    sends = [swap(coded(part[k - 1], norms[k]), "proj", n_p, 2 * k) for k in range(1, n_z)]
    total = then(own_part[near])[0] + decode(codes[1], product_gain)
    norms = norms[0]
    for code in sends:
        got, got_norms = decoded(code, own)
        total, norms = total + got, norms + got_norms

    factor = float(width * n_g) ** 0.5
    scores = factor * total * lax.rsqrt(norms[0, :own] + EPS)[:, None] * lax.rsqrt(norms[1] + EPS)[None, :]
    blocks = jnp.split(scores, 2 * in_chunk, axis=1)
    swapped = jnp.concatenate([blocks[n ^ 1] for n in range(2 * in_chunk)], axis=1)
    return jnp.where(py == 0, scores, swapped)


def solution(mesh):
    n_p, n_g = mesh.shape["proj"], mesh.shape["grp"]

    def body(grads, proj_matrix, targets):
        return per_device(n_p, n_g, grads, proj_matrix, targets)

    placed = (P("grp", "proj"), P("proj", "grp"), P("proj", "grp"))
    return jax.shard_map(
        body, mesh=mesh, in_specs=placed, out_specs=P("proj", "grp"), check_vma=False
    )
```

time: 364 us -> 125 us (0.34)
  waiting for transfers between devices: 315 us -> 58.8 us
  starting transfers between devices: 0.12 us -> 30.1 us
  between operations: 13.1 us -> 0.8 us
  blocking collectives: 7.13 us -> 0 us
    reduce_scatter x2 -> x0, waiting for transfers between devices: 162 us -> none  [the longest x1 151 us: per_device(): lax.psum_scatter(jnp.dot(gathered, proj_matrix, preferred_element_type=jn...]
    all_gather x2 -> x0, waiting for transfers between devices: 151 us -> none  [the longest x1 113 us: per_device(): target_all = lax.all_gather(targets, 'proj', axis=0, tiled=True)]
    ppermute x0 -> x26, waiting for transfers between devices: none -> 58.8 us  [swap(): return lax.ppermute(value, axis, [(i, i ^ bit) for i in range(size)])]
    ppermute x0 -> x26, starting transfers between devices: none -> 30.1 us  [swap(): return lax.ppermute(value, axis, [(i, i ^ bit) for i in range(size)])]
    dot_general x1 -> x6, matrix products: 14.4 us -> 22.5 us  [the longest x2 12.2 us: partial(): part = done(jnp.dot(then(chunk), proj_matrix, preferred_element_type=F32))]
    psum x1 -> x0, blocking collectives: 7.13 us -> none  [per_device(): feature_sq, target_sq = lax.psum((feature_sq, target_sq), 'grp')]
    dot_general x1 -> x4, matrix products: 7.73 us -> 1.9 us  [inner_rows(): lax.dot_general(left, right, (((1,), (1,)), ((), ())), preferred_element_...]
    reduce_sum x2 -> x3, other arithmetic: 5.23 us -> 0.74 us  [the longest x2 0.56 us: per_device(): jnp.sum(jnp.square(value.astype(F32)), axis=2)]
  transfers between devices with their start and end apart: 4 -> 26, of which waited for: 4 -> 13; matrix products, arithmetic and copies ran while one was open for 5% -> 27% of each run, Pallas kernels for 0% -> 0%
where the time goes in v2:
time: 125 us
  waiting for transfers between devices  58.8 us (47%)
  starting transfers between devices  30.1 us (24%)
  matrix products  24.4 us (20%)
  other arithmetic  9.86 us (8%)
    ppermute x26, waiting for transfers between devices, swap(): return lax.ppermute(value, axis, [(i, i ^ bit) for i in range(size)])  58.8 us
    ppermute x26, starting transfers between devices, swap(): return lax.ppermute(value, axis, [(i, i ^ bit) for i in range(size)])  30.1 us
    dot_general x2, matrix products, partial(): part = done(jnp.dot(then(chunk), proj_matrix, preferred_element_type=F32))  12.2 us
    dot_general x2, matrix products, partial_away(): jnp.dot(then(side(chunk, 1 - py)), proj_matrix, preferred_element_type=F32)  6.7 us
    dot_general x2, matrix products, partial_kept(): jnp.dot(then(side(chunk, py)), proj_matrix, preferred_element_type=F32)  3.68 us
    add x8, other arithmetic, collect(): return done(then(kept[i]) + decode(code[i], feature_gain))  2.56 us
  transfers between devices with their start and end apart: 26, of which 13 were waited for; matrix products, arithmetic and copies ran while one was open for 27% of the time, Pallas kernels for 0%

profile of v2, /device:TPU:0, one launch (start us, length us, event | category | flops | bytes accessed | tf_op | source)
XLA Modules:
  0.0 124.7 jit_solution(18281908243163618489)
XLA Ops:
  0.5 2.5 %collective-permute-start.2 = (bf16[256,2048]{1,0:T(8,128)(2,1)}, bf16[256,2048]{1,0:T(8,128)(2,1)}, u32[]{:S(2)}, u32[]{:S(2)}) collective-permute-start(bf16[256,2048]{1,0:T(8,128)(2,1)} %param.3), channel_id=1, source_target_pairs={{0,2},{1,3},{2,0},{3,1},{4,6},{5,7},{6,4},{7,5},{8,10},{9,11},{10,... | collective-permute-start | bytes 3145736 | tf_op jit(solution)/shard_map/ppermute | solution.py:13
  2.9 6.1 %fusion.129 = f32[256,2048]{1,0:T(8,128)S(1)} fusion(bf16[256,2048]{1,0:T(8,128)(2,1)} %param.3, bf16[2048,2048]{1,0:T(8,128)(2,1)} %param.4), kind=kOutput, calls=%fused_computation.301 | convolution fusion | flops 2147483648 | bytes 11534336 | tf_op jit(solution)/shard_map/dot_general | solution.py:97
  11.9 2.7 %collective-permute-start.7 = (bf16[1,256,1024]{2,1,0:T(8,128)(2,1)S(1)}, bf16[1,256,1024]{2,1,0:T(8,128)(2,1)}, u32[]{:S(2)}, u32[]{:S(2)}) collective-permute-start(bf16[1,256,1024]{2,1,0:T(8,128)(2,1)S(1)} %get-tuple-element.36), channel_id=1, source_target_pairs={{0,16},{4,20},{8,24},{12,28},{16,0},{20,4},{24,8},{28,12},{1,17},{... | collective-permute-start | bytes 1572872 | tf_op jit(solution)/shard_map/ppermute | solution.py:13
  14.7 6.0 %fusion.16 = f32[256,2048]{1,0:T(8,128)S(1)} fusion(bf16[2048,2048]{1,0:T(8,128)(2,1)} %param.4, bf16[256,2048]{1,0:T(8,128)(2,1)} %collective-permute-done, bf16[2048]{0:T(1024)(128)(2,1)S(1)} %fusion.103), kind=kOutput, calls=%fused_computation.47 | convolution fusion | flops 2148007936 | bytes 11538432 | tf_op jit(solution)/shard_map/dot_general | solution.py:97
  20.7 3.8 %collective-permute-done.1 = f16[128,2048]{1,0:T(8,128)(2,1)} collective-permute-done((f16[128,2048]{1,0:T(8,128)(2,1)}, f16[128,2048]{1,0:T(8,128)(2,1)}, u32[]{:S(2)}, u32[]{:S(2)}) %collective-permute-start.1) | collective-permute-done | bytes 524320 | tf_op jit(solution)/shard_map/ppermute | solution.py:13
  26.0 1.6 %collective-permute-start.6 = (f16[2,128,512]{2,1,0:T(8,128)(2,1)S(1)}, f16[2,128,512]{2,1,0:T(8,128)(2,1)S(1)}, u32[]{:S(2)}, u32[]{:S(2)}) collective-permute-start(f16[2,128,512]{2,1,0:T(8,128)(2,1)S(1)} %multiply_convert_fusion.5), channel_id=1, source_target_pairs={{0,8},{4,12},{8,0},{12,4},{16,24},{20,28},{24,16},{28,20},{1,9},{5... | collective-permute-start | bytes 786440 | tf_op jit(solution)/shard_map/ppermute | solution.py:13
  29.5 5.1 %multiply_convert_fusion.1 = (f16[128,2048]{1,0:T(8,128)(2,1)S(1)}, f32[128,2048]{1,0:T(8,128)S(1)}) fusion(bf16[2048,2048]{1,0:T(8,128)(2,1)} %param.4, bf16[1,2,128,2048]{3,2,1,0:T(8,128)(2,1)} %bitcast.6, s32[]{:T(128)S(6)} %select_n.147, bf16[2048]{0:T(1024)(128)(2,1)S(1)} %fusion.104), kind=kOutput, calls=%fused_computation.45 | convolution fusion | flops 1075314688 | bytes 10489860 | tf_op jit(solution)/shard_map/dot_general | solution.py:102
  35.5 7.3 %collective-permute-done.3 = f16[128,2048]{1,0:T(8,128)(2,1)S(1)} collective-permute-done((f16[128,2048]{1,0:T(8,128)(2,1)S(1)}, f16[128,2048]{1,0:T(8,128)(2,1)S(1)}, u32[]{:S(2)}, u32[]{:S(2)}) %collective-permute-start.3) | collective-permute-done | bytes 524320 | tf_op jit(solution)/shard_map/ppermute | solution.py:13
  43.8 2.4 %fusion.45 = f32[128,2048]{1,0:T(8,128)S(1)} fusion(bf16[2048,2048]{1,0:T(8,128)(2,1)S(1)} %bitcast.197, bf16[1,2,128,2048]{3,2,1,0:T(8,128)(2,1)} %bitcast.6, s32[]{:T(128)S(6)} %select_n.146, bf16[2048]{0:T(1024)(128)(2,1)S(1)} %fusion.105), kind=kOutput, calls=%fused_computation.101 | convolution fusion | flops 1074003968 | bytes 9965572 | tf_op jit(solution)/shard_map/dot_general | solution.py:106
  47.5 1.6 %collective-permute-start.16 = (bf16[2,256,512]{2,1,0:T(8,128)(2,1)S(1)}, bf16[2,256,512]{2,1,0:T(8,128)(2,1)S(1)}, u32[]{:S(2)}, u32[]{:S(2)}) collective-permute-start(bf16[2,256,512]{2,1,0:T(8,128)(2,1)S(1)} %get-tuple-element.34), channel_id=1, source_target_pairs={{0,8},{4,12},{8,0},{12,4},{16,24},{20,28},{24,16},{28,20},{1,9},{5... | collective-permute-start | bytes 1572872 | tf_op jit(solution)/shard_map/ppermute | solution.py:13
  49.1 4.9 %collective-permute-done.8 = f16[2,128,512]{2,1,0:T(8,128)(2,1)S(1)} collective-permute-done((f16[2,128,512]{2,1,0:T(8,128)(2,1)S(1)}, f16[2,128,512]{2,1,0:T(8,128)(2,1)S(1)}, u32[]{:S(2)}, u32[]{:S(2)}) %collective-permute-start.8) | collective-permute-done | bytes 262176 | tf_op jit(solution)/shard_map/ppermute | solution.py:13
  58.9 1.9 %collective-permute-start.9 = (f16[1,128,512]{2,1,0:T(8,128)(2,1)S(1)}, f16[1,128,512]{2,1,0:T(8,128)(2,1)S(1)}, u32[]{:S(2)}, u32[]{:S(2)}) collective-permute-start(f16[1,128,512]{2,1,0:T(8,128)(2,1)S(1)} %multiply_convert_fusion.13), channel_id=1, source_target_pairs={{0,16},{4,20},{8,24},{12,28},{16,0},{20,4},{24,8},{28,12},{1,17},{... | collective-permute-start | bytes 393224 | tf_op jit(solution)/shard_map/ppermute | solution.py:13
  62.3 3.5 %collective-permute-done.16 = bf16[2,256,512]{2,1,0:T(8,128)(2,1)S(1)} collective-permute-done((bf16[2,256,512]{2,1,0:T(8,128)(2,1)S(1)}, bf16[2,256,512]{2,1,0:T(8,128)(2,1)S(1)}, u32[]{:S(2)}, u32[]{:S(2)}) %collective-permute-start.16) | collective-permute-done | bytes 524320 | tf_op jit(solution)/shard_map/ppermute | solution.py:13
  65.9 1.8 %collective-permute-start.17 = (bf16[4,256,512]{2,1,0:T(8,128)(2,1)S(1)}, bf16[4,256,512]{2,1,0:T(8,128)(2,1)S(1)}, u32[]{:S(2)}, u32[]{:S(2)}) collective-permute-start(bf16[4,256,512]{2,1,0:T(8,128)(2,1)S(1)} %pad_maximum_fusion), channel_id=1, source_target_pairs={{0,4},{4,0},{8,12},{12,8},{16,20},{20,16},{24,28},{28,24},{1,5},{5... | collective-permute-start | bytes 3145736 | tf_op jit(solution)/shard_map/ppermute | solution.py:13
  68.4 7.2 %collective-permute-done.12 = f16[128,2048]{1,0:T(8,128)(2,1)S(1)} collective-permute-done((f16[128,2048]{1,0:T(8,128)(2,1)S(1)}, f16[128,2048]{1,0:T(8,128)(2,1)S(1)}, u32[]{:S(2)}, u32[]{:S(2)}) %collective-permute-start.12) | collective-permute-done | bytes 524320 | tf_op jit(solution)/shard_map/ppermute | solution.py:13
  76.7 1.8 %collective-permute-start.13 = (f16[2,128,512]{2,1,0:T(8,128)(2,1)S(1)}, f16[2,128,512]{2,1,0:T(8,128)(2,1)S(1)}, u32[]{:S(2)}, u32[]{:S(2)}) collective-permute-start(f16[2,128,512]{2,1,0:T(8,128)(2,1)S(1)} %multiply_convert_fusion.2), channel_id=1, source_target_pairs={{0,8},{4,12},{8,0},{12,4},{16,24},{20,28},{24,16},{28,20},{1,9},{5... | collective-permute-start | bytes 786440 | tf_op jit(solution)/shard_map/ppermute | solution.py:13
  78.5 4.1 %collective-permute-done.10 = f16[2,128,512]{2,1,0:T(8,128)(2,1)S(1)} collective-permute-done((f16[2,128,512]{2,1,0:T(8,128)(2,1)S(1)}, f16[2,128,512]{2,1,0:T(8,128)(2,1)S(1)}, u32[]{:S(2)}, u32[]{:S(2)}) %collective-permute-start.10) | collective-permute-done | bytes 262176 | tf_op jit(solution)/shard_map/ppermute | solution.py:13
  83.2 2.2 %collective-permute-done.13 = f16[2,128,512]{2,1,0:T(8,128)(2,1)S(1)} collective-permute-done((f16[2,128,512]{2,1,0:T(8,128)(2,1)S(1)}, f16[2,128,512]{2,1,0:T(8,128)(2,1)S(1)}, u32[]{:S(2)}, u32[]{:S(2)}) %collective-permute-start.13) | collective-permute-done | bytes 262176 | tf_op jit(solution)/shard_map/ppermute | solution.py:13
  86.1 3.7 %collective-permute-done.14 = f16[1,128,512]{2,1,0:T(8,128)(2,1)S(1)} collective-permute-done((f16[1,128,512]{2,1,0:T(8,128)(2,1)S(1)}, f16[1,128,512]{2,1,0:T(8,128)(2,1)S(1)}, u32[]{:S(2)}, u32[]{:S(2)}) %collective-permute-start.14) | collective-permute-done | bytes 131104 | tf_op jit(solution)/shard_map/ppermute | solution.py:13
  89.9 2.7 %collective-permute-done.15 = f16[1,128,512]{2,1,0:T(8,128)(2,1)S(1)} collective-permute-done((f16[1,128,512]{2,1,0:T(8,128)(2,1)S(1)}, f16[1,128,512]{2,1,0:T(8,128)(2,1)S(1)}, u32[]{:S(2)}, u32[]{:S(2)}) %collective-permute-start.15) | collective-permute-done | bytes 131104 | tf_op jit(solution)/shard_map/ppermute | solution.py:13
  100.0 9.7 %collective-permute-done.21 = f16[400,512]{1,0:T(8,128)(2,1)S(1)} collective-permute-done((f16[400,512]{1,0:T(8,128)(2,1)S(1)}, f16[400,512]{1,0:T(8,128)(2,1)S(1)}, u32[]{:S(2)}, u32[]{:S(2)}) %collective-permute-start.21) | collective-permute-done | bytes 409632 | tf_op jit(solution)/shard_map/ppermute | solution.py:13
  110.4 2.5 %collective-permute-start.24 = (f16[144,512]{1,0:T(8,128)(2,1)S(1)}, f16[144,512]{1,0:T(8,128)(2,1)S(1)}, u32[]{:S(2)}, u32[]{:S(2)}) collective-permute-start(f16[144,512]{1,0:T(8,128)(2,1)S(1)} %pad_maximum_fusion.10), channel_id=1, source_target_pairs={{0,16},{4,20},{8,24},{12,28},{16,0},{20,4},{24,8},{28,12},{1,17},{... | collective-permute-start | bytes 442376 | tf_op jit(solution)/shard_map/ppermute | solution.py:13
  113.0 2.0 %collective-permute-start.25 = (f16[144,512]{1,0:T(8,128)(2,1)S(1)}, f16[144,512]{1,0:T(8,128)(2,1)S(1)}, u32[]{:S(2)}, u32[]{:S(2)}) collective-permute-start(f16[144,512]{1,0:T(8,128)(2,1)S(1)} %pad_maximum_fusion.11), channel_id=1, source_target_pairs={{0,24},{4,28},{8,16},{12,20},{16,8},{20,12},{24,0},{28,4},{1,25},{... | collective-permute-start | bytes 442376 | tf_op jit(solution)/shard_map/ppermute | solution.py:13
  116.6 7.0 %collective-permute-done.24 = f16[144,512]{1,0:T(8,128)(2,1)S(1)} collective-permute-done((f16[144,512]{1,0:T(8,128)(2,1)S(1)}, f16[144,512]{1,0:T(8,128)(2,1)S(1)}, u32[]{:S(2)}, u32[]{:S(2)}) %collective-permute-start.24) | collective-permute-done | bytes 147488 | tf_op jit(solution)/shard_map/ppermute | solution.py:13
  (141 shorter events, 29.7 us)
Async XLA Ops:
  0.0 14.6 %collective-permute-start = (bf16[256,2048]{1,0:T(8,128)(2,1)}, bf16[256,2048]{1,0:T(8,128)(2,1)}, u32[]{:S(2)}, u32[]{:S(2)}) collective-permute-start(bf16[256,2048]{1,0:T(8,128)(2,1)} %param.3), channel_id=1, source_target_pairs={{0,1},{1,0},{2,3},{3,2},{4,5},{5,4},{6,7},{7,6},{8,9},{9,8},{10,11... | collective-permute-start | bytes 3145736 | tf_op jit(solution)/shard_map/ppermute | solution.py:13
  0.5 29.0 %collective-permute-start.2 = (bf16[256,2048]{1,0:T(8,128)(2,1)}, bf16[256,2048]{1,0:T(8,128)(2,1)}, u32[]{:S(2)}, u32[]{:S(2)}) collective-permute-start(bf16[256,2048]{1,0:T(8,128)(2,1)} %param.3), channel_id=1, source_target_pairs={{0,2},{1,3},{2,0},{3,1},{4,6},{5,7},{6,4},{7,5},{8,10},{9,11},{10,... | collective-permute-start | bytes 3145736 | tf_op jit(solution)/shard_map/ppermute | solution.py:13
  10.1 14.4 %collective-permute-start.1 = (f16[128,2048]{1,0:T(8,128)(2,1)}, f16[128,2048]{1,0:T(8,128)(2,1)}, u32[]{:S(2)}, u32[]{:S(2)}) collective-permute-start(f16[128,2048]{1,0:T(8,128)(2,1)} %fusion.15), channel_id=1, source_target_pairs={{0,4},{4,0},{8,12},{12,8},{16,20},{20,16},{24,28},{28,24},{1,5},{5... | collective-permute-start | bytes 1572872 | tf_op jit(solution)/shard_map/ppermute | solution.py:13
  11.9 34.3 %collective-permute-start.7 = (bf16[1,256,1024]{2,1,0:T(8,128)(2,1)S(1)}, bf16[1,256,1024]{2,1,0:T(8,128)(2,1)}, u32[]{:S(2)}, u32[]{:S(2)}) collective-permute-start(bf16[1,256,1024]{2,1,0:T(8,128)(2,1)S(1)} %get-tuple-element.36), channel_id=1, source_target_pairs={{0,16},{4,20},{8,24},{12,28},{16,0},{20,4},{24,8},{28,12},{1,17},{... | collective-permute-start | bytes 1572872 | tf_op jit(solution)/shard_map/ppermute | solution.py:13
  26.0 32.6 %collective-permute-start.6 = (f16[2,128,512]{2,1,0:T(8,128)(2,1)S(1)}, f16[2,128,512]{2,1,0:T(8,128)(2,1)S(1)}, u32[]{:S(2)}, u32[]{:S(2)}) collective-permute-start(f16[2,128,512]{2,1,0:T(8,128)(2,1)S(1)} %multiply_convert_fusion.5), channel_id=1, source_target_pairs={{0,8},{4,12},{8,0},{12,4},{16,24},{20,28},{24,16},{28,20},{1,9},{5... | collective-permute-start | bytes 786440 | tf_op jit(solution)/shard_map/ppermute | solution.py:13
  27.9 14.9 %collective-permute-start.3 = (f16[128,2048]{1,0:T(8,128)(2,1)S(1)}, f16[128,2048]{1,0:T(8,128)(2,1)S(1)}, u32[]{:S(2)}, u32[]{:S(2)}) collective-permute-start(f16[128,2048]{1,0:T(8,128)(2,1)S(1)} %fusion.11), channel_id=1, source_target_pairs={{0,4},{4,0},{8,12},{12,8},{16,20},{20,16},{24,28},{28,24},{1,5},{5... | collective-permute-start | bytes 1572872 | tf_op jit(solution)/shard_map/ppermute | solution.py:13
  34.6 23.6 %collective-permute-start.5 = (f16[128,2048]{1,0:T(8,128)(2,1)S(1)}, f16[128,2048]{1,0:T(8,128)(2,1)S(1)}, u32[]{:S(2)}, u32[]{:S(2)}) collective-permute-start(f16[128,2048]{1,0:T(8,128)(2,1)S(1)} %get-tuple-element.64), channel_id=1, source_target_pairs={{0,4},{4,0},{8,12},{12,8},{16,20},{20,16},{24,28},{28,24},{1,5},{5... | collective-permute-start | bytes 1572872 | tf_op jit(solution)/shard_map/ppermute | solution.py:13
  35.5 19.8 %collective-permute-start.4 = (bf16[256,2048]{1,0:T(8,128)(2,1)}, bf16[256,2048]{1,0:T(8,128)(2,1)S(1)}, u32[]{:S(2)}, u32[]{:S(2)}) collective-permute-start(bf16[256,2048]{1,0:T(8,128)(2,1)} %collective-permute-done.2), channel_id=1, source_target_pairs={{0,1},{1,0},{2,3},{3,2},{4,5},{5,4},{6,7},{7,6},{8,9},{9,8},{10,11... | collective-permute-start | bytes 3145736 | tf_op jit(solution)/shard_map/ppermute | solution.py:13
  43.3 10.7 %collective-permute-start.8 = (f16[2,128,512]{2,1,0:T(8,128)(2,1)S(1)}, f16[2,128,512]{2,1,0:T(8,128)(2,1)S(1)}, u32[]{:S(2)}, u32[]{:S(2)}) collective-permute-start(f16[2,128,512]{2,1,0:T(8,128)(2,1)S(1)} %multiply_convert_fusion.4), channel_id=1, source_target_pairs={{0,8},{4,12},{8,0},{12,4},{16,24},{20,28},{24,16},{28,20},{1,9},{5... | collective-permute-start | bytes 786440 | tf_op jit(solution)/shard_map/ppermute | solution.py:13
  47.5 18.3 %collective-permute-start.16 = (bf16[2,256,512]{2,1,0:T(8,128)(2,1)S(1)}, bf16[2,256,512]{2,1,0:T(8,128)(2,1)S(1)}, u32[]{:S(2)}, u32[]{:S(2)}) collective-permute-start(bf16[2,256,512]{2,1,0:T(8,128)(2,1)S(1)} %get-tuple-element.34), channel_id=1, source_target_pairs={{0,8},{4,12},{8,0},{12,4},{16,24},{20,28},{24,16},{28,20},{1,9},{5... | collective-permute-start | bytes 1572872 | tf_op jit(solution)/shard_map/ppermute | solution.py:13
  54.2 28.9 %collective-permute-start.11 = (f16[1,128,512]{2,1,0:T(8,128)(2,1)S(1)}, f16[1,128,512]{2,1,0:T(8,128)(2,1)S(1)}, u32[]{:S(2)}, u32[]{:S(2)}) collective-permute-start(f16[1,128,512]{2,1,0:T(8,128)(2,1)S(1)} %multiply_convert_fusion.12), channel_id=1, source_target_pairs={{0,16},{4,20},{8,24},{12,28},{16,0},{20,4},{24,8},{28,12},{1,17},{... | collective-permute-start | bytes 393224 | tf_op jit(solution)/shard_map/ppermute | solution.py:13
  58.9 17.6 %collective-permute-start.9 = (f16[1,128,512]{2,1,0:T(8,128)(2,1)S(1)}, f16[1,128,512]{2,1,0:T(8,128)(2,1)S(1)}, u32[]{:S(2)}, u32[]{:S(2)}) collective-permute-start(f16[1,128,512]{2,1,0:T(8,128)(2,1)S(1)} %multiply_convert_fusion.13), channel_id=1, source_target_pairs={{0,16},{4,20},{8,24},{12,28},{16,0},{20,4},{24,8},{28,12},{1,17},{... | collective-permute-start | bytes 393224 | tf_op jit(solution)/shard_map/ppermute | solution.py:13
  60.8 14.8 %collective-permute-start.12 = (f16[128,2048]{1,0:T(8,128)(2,1)S(1)}, f16[128,2048]{1,0:T(8,128)(2,1)S(1)}, u32[]{:S(2)}, u32[]{:S(2)}) collective-permute-start(f16[128,2048]{1,0:T(8,128)(2,1)S(1)} %get-tuple-element.62), channel_id=1, source_target_pairs={{0,4},{4,0},{8,12},{12,8},{16,20},{20,16},{24,28},{28,24},{1,5},{5... | collective-permute-start | bytes 1572872 | tf_op jit(solution)/shard_map/ppermute | solution.py:13
  65.9 27.1 %collective-permute-start.17 = (bf16[4,256,512]{2,1,0:T(8,128)(2,1)S(1)}, bf16[4,256,512]{2,1,0:T(8,128)(2,1)S(1)}, u32[]{:S(2)}, u32[]{:S(2)}) collective-permute-start(bf16[4,256,512]{2,1,0:T(8,128)(2,1)S(1)} %pad_maximum_fusion), channel_id=1, source_target_pairs={{0,4},{4,0},{8,12},{12,8},{16,20},{20,16},{24,28},{28,24},{1,5},{5... | collective-permute-start | bytes 3145736 | tf_op jit(solution)/shard_map/ppermute | solution.py:13
  76.1 6.4 %collective-permute-start.10 = (f16[2,128,512]{2,1,0:T(8,128)(2,1)S(1)}, f16[2,128,512]{2,1,0:T(8,128)(2,1)S(1)}, u32[]{:S(2)}, u32[]{:S(2)}) collective-permute-start(f16[2,128,512]{2,1,0:T(8,128)(2,1)S(1)} %multiply_convert_fusion.3), channel_id=1, source_target_pairs={{0,8},{4,12},{8,0},{12,4},{16,24},{20,28},{24,16},{28,20},{1,9},{5... | collective-permute-start | bytes 786440 | tf_op jit(solution)/shard_map/ppermute | solution.py:13
  76.7 8.7 %collective-permute-start.13 = (f16[2,128,512]{2,1,0:T(8,128)(2,1)S(1)}, f16[2,128,512]{2,1,0:T(8,128)(2,1)S(1)}, u32[]{:S(2)}, u32[]{:S(2)}) collective-permute-start(f16[2,128,512]{2,1,0:T(8,128)(2,1)S(1)} %multiply_convert_fusion.2), channel_id=1, source_target_pairs={{0,8},{4,12},{8,0},{12,4},{16,24},{20,28},{24,16},{28,20},{1,9},{5... | collective-permute-start | bytes 786440 | tf_op jit(solution)/shard_map/ppermute | solution.py:13
  82.8 7.1 %collective-permute-start.14 = (f16[1,128,512]{2,1,0:T(8,128)(2,1)S(1)}, f16[1,128,512]{2,1,0:T(8,128)(2,1)S(1)}, u32[]{:S(2)}, u32[]{:S(2)}) collective-permute-start(f16[1,128,512]{2,1,0:T(8,128)(2,1)S(1)} %multiply_convert_fusion.11), channel_id=1, source_target_pairs={{0,16},{4,20},{8,24},{12,28},{16,0},{20,4},{24,8},{28,12},{1,17},{... | collective-permute-start | bytes 393224 | tf_op jit(solution)/shard_map/ppermute | solution.py:13
  85.6 7.1 %collective-permute-start.15 = (f16[1,128,512]{2,1,0:T(8,128)(2,1)S(1)}, f16[1,128,512]{2,1,0:T(8,128)(2,1)S(1)}, u32[]{:S(2)}, u32[]{:S(2)}) collective-permute-start(f16[1,128,512]{2,1,0:T(8,128)(2,1)S(1)} %multiply_convert_fusion.10), channel_id=1, source_target_pairs={{0,16},{4,20},{8,24},{12,28},{16,0},{20,4},{24,8},{28,12},{1,17},{... | collective-permute-start | bytes 393224 | tf_op jit(solution)/shard_map/ppermute | solution.py:13
  95.1 4.4 %collective-permute-start.18 = (f32[4,128,512]{2,1,0:T(8,128)S(1)}, f32[4,128,512]{2,1,0:T(8,128)S(1)}, u32[]{:S(2)}, u32[]{:S(2)}) collective-permute-start(f32[4,128,512]{2,1,0:T(8,128)S(1)} %convolution_add_fusion.1), channel_id=1, source_target_pairs={{0,1},{1,0},{2,3},{3,2},{4,5},{5,4},{6,7},{7,6},{8,9},{9,8},{10,11... | collective-permute-start | bytes 3145736 | tf_op jit(solution)/shard_map/ppermute | solution.py:13
  97.3 12.4 %collective-permute-start.21 = (f16[400,512]{1,0:T(8,128)(2,1)S(1)}, f16[400,512]{1,0:T(8,128)(2,1)S(1)}, u32[]{:S(2)}, u32[]{:S(2)}) collective-permute-start(f16[400,512]{1,0:T(8,128)(2,1)S(1)} %pad_maximum_fusion.8), channel_id=1, source_target_pairs={{0,2},{1,3},{2,0},{3,1},{4,6},{5,7},{6,4},{7,5},{8,10},{9,11},{10,... | collective-permute-start | bytes 1228808 | tf_op jit(solution)/shard_map/ppermute | solution.py:13
  97.9 25.8 %collective-permute-start.22 = (f16[128,512]{1,0:T(8,128)(2,1)S(1)}, f16[128,512]{1,0:T(8,128)(2,1)S(1)}, u32[]{:S(2)}, u32[]{:S(2)}) collective-permute-start(f16[128,512]{1,0:T(8,128)(2,1)S(1)} %multiply_convert_fusion.9), channel_id=1, source_target_pairs={{0,2},{1,3},{2,0},{3,1},{4,6},{5,7},{6,4},{7,5},{8,10},{9,11},{10,... | collective-permute-start | bytes 393224 | tf_op jit(solution)/shard_map/ppermute | solution.py:13
  110.3 6.3 %collective-permute-start.23 = (f16[144,512]{1,0:T(8,128)(2,1)S(1)}, f16[144,512]{1,0:T(8,128)(2,1)S(1)}, u32[]{:S(2)}, u32[]{:S(2)}) collective-permute-start(f16[144,512]{1,0:T(8,128)(2,1)S(1)} %pad_maximum_fusion.9), channel_id=1, source_target_pairs={{0,8},{4,12},{8,0},{12,4},{16,24},{20,28},{24,16},{28,20},{1,9},{5... | collective-permute-start | bytes 442376 | tf_op jit(solution)/shard_map/ppermute | solution.py:13
  110.4 13.2 %collective-permute-start.24 = (f16[144,512]{1,0:T(8,128)(2,1)S(1)}, f16[144,512]{1,0:T(8,128)(2,1)S(1)}, u32[]{:S(2)}, u32[]{:S(2)}) collective-permute-start(f16[144,512]{1,0:T(8,128)(2,1)S(1)} %pad_maximum_fusion.10), channel_id=1, source_target_pairs={{0,16},{4,20},{8,24},{12,28},{16,0},{20,4},{24,8},{28,12},{1,17},{... | collective-permute-start | bytes 442376 | tf_op jit(solution)/shard_map/ppermute | solution.py:13
  113.0 10.6 %collective-permute-start.25 = (f16[144,512]{1,0:T(8,128)(2,1)S(1)}, f16[144,512]{1,0:T(8,128)(2,1)S(1)}, u32[]{:S(2)}, u32[]{:S(2)}) collective-permute-start(f16[144,512]{1,0:T(8,128)(2,1)S(1)} %pad_maximum_fusion.11), channel_id=1, source_target_pairs={{0,24},{4,28},{8,16},{12,20},{16,8},{20,12},{24,0},{28,4},{1,25},{... | collective-permute-start | bytes 442376 | tf_op jit(solution)/shard_map/ppermute | solution.py:13
  (5 other events, 44.4 us)

commit v3 on v2

--- a/solution.py
+++ b/solution.py
@@ -93,11 +93,6 @@
 
     kept, code, features = {}, {}, {}
 
-    def partial(i, chunk):
-        part = done(jnp.dot(then(chunk), proj_matrix, preferred_element_type=F32))
-        kept[i] = side(part, py)
-        code[i] = swap(encode(side(part, 1 - py), feature_gain), "proj", n_p, 1)
-
     def partial_away(i, chunk):
         part = done(jnp.dot(then(side(chunk, 1 - py)), proj_matrix, preferred_element_type=F32))
         code[i] = swap(encode(part, feature_gain), "proj", n_p, 1)
@@ -129,11 +124,13 @@
     grads_2 = swap(grads, "grp", n_g, 2)
     grads_1 = swap(grads, "grp", n_g, 1)
 
-    step(partial, 0, grads)
+    step(partial_away, 0, grads)
     grads_3 = swap(grads_2, "grp", n_g, 1)
     tgt = step(targets_over_z, targets[None], z_bits[-1])
-    step(partial, 1, grads_1)
+    step(partial_away, 1, grads_1)
+    step(partial_kept, 0, grads)
     step(spread, 0, 1)
+    step(partial_kept, 1, grads_1)
     step(partial_away, 2, grads_2)
     step(spread, 1, 1)
     step(partial_kept, 2, grads_2)

time: 125 us -> 123 us (0.984)
  waiting for transfers between devices: 58.8 us -> 52.9 us
  starting transfers between devices: 30.1 us -> 34 us
    dot_general x2 -> x0, matrix products: 12.2 us -> none  [partial(): part = done(jnp.dot(then(chunk), proj_matrix, preferred_element_type=F32))]
    dot_general x2 -> x4, matrix products: 6.7 us -> 13.8 us  [partial_away(): jnp.dot(then(side(chunk, 1 - py)), proj_matrix, preferred_element_type=F32)]
    ppermute x26, waiting for transfers between devices: 58.8 us -> 52.9 us  [swap(): return lax.ppermute(value, axis, [(i, i ^ bit) for i in range(size)])]
    dot_general x2 -> x4, matrix products: 3.68 us -> 9.08 us  [partial_kept(): jnp.dot(then(side(chunk, py)), proj_matrix, preferred_element_type=F32)]
    ppermute x26, starting transfers between devices: 30.1 us -> 34 us  [swap(): return lax.ppermute(value, axis, [(i, i ^ bit) for i in range(size)])]
    convert_element_type x17 -> x15, other arithmetic: 2.49 us -> 1.22 us  [encode(): (value * (lax.rsqrt(jnp.maximum(jnp.abs(value), 1e-35)) * gain)).astype(F16)]
  transfers between devices with their start and end apart: 26 -> 26, of which waited for: 13 -> 12; matrix products, arithmetic and copies ran while one was open for 27% -> 27% of each run, Pallas kernels for 0% -> 0%
where the time goes in v3:
time: 123 us
  waiting for transfers between devices  52.9 us (43%)
  starting transfers between devices  34 us (28%)
  matrix products  24.8 us (20%)
  other arithmetic  9.64 us (8%)
    ppermute x26, waiting for transfers between devices, swap(): return lax.ppermute(value, axis, [(i, i ^ bit) for i in range(size)])  52.9 us
    ppermute x26, starting transfers between devices, swap(): return lax.ppermute(value, axis, [(i, i ^ bit) for i in range(size)])  34 us
    dot_general x4, matrix products, partial_away(): jnp.dot(then(side(chunk, 1 - py)), proj_matrix, preferred_element_type=F32)  13.8 us
    dot_general x4, matrix products, partial_kept(): jnp.dot(then(side(chunk, py)), proj_matrix, preferred_element_type=F32)  9.08 us
  transfers between devices with their start and end apart: 26, of which 12 were waited for; matrix products, arithmetic and copies ran while one was open for 27% of the time, Pallas kernels for 0%

profile of v3, /device:TPU:0, one launch (start us, length us, event | category | flops | bytes accessed | tf_op | source)
XLA Modules:
  0.0 122.8 jit_solution(13919855997417097753)
XLA Ops:
  0.5 2.5 %collective-permute-start.2 = (bf16[256,2048]{1,0:T(8,128)(2,1)}, bf16[256,2048]{1,0:T(8,128)(2,1)S(1)}, u32[]{:S(2)}, u32[]{:S(2)}) collective-permute-start(bf16[256,2048]{1,0:T(8,128)(2,1)} %param.3), channel_id=1, source_target_pairs={{0,2},{1,3},{2,0},{3,1},{4,6},{5,7},{6,4},{7,5},{8,10},{9,11},{10,... | collective-permute-start | bytes 3145736 | tf_op jit(solution)/shard_map/ppermute | solution.py:13
  2.9 5.8 %multiply_convert_fusion.3 = (f16[128,2048]{1,0:T(8,128)(2,1)}, f32[128,2048]{1,0:T(8,128)S(1)}) fusion(bf16[2048,2048]{1,0:T(8,128)(2,1)} %param.4, bf16[1,2,128,2048]{3,2,1,0:T(8,128)(2,1)} %bitcast.182, s32[]{:T(128)S(6)} %select_n.146), kind=kOutput, calls=%fused_computation.34 | convolution fusion | flops 1075052544 | bytes 10485764 | tf_op jit(solution)/shard_map/dot_general | solution.py:97
  11.7 2.7 %collective-permute-start.7 = (bf16[1,256,1024]{2,1,0:T(8,128)(2,1)S(1)}, bf16[1,256,1024]{2,1,0:T(8,128)(2,1)}, u32[]{:S(2)}, u32[]{:S(2)}) collective-permute-start(bf16[1,256,1024]{2,1,0:T(8,128)(2,1)S(1)} %get-tuple-element.36), channel_id=1, source_target_pairs={{0,16},{4,20},{8,24},{12,28},{16,0},{20,4},{24,8},{28,12},{1,17},{... | collective-permute-start | bytes 1572872 | tf_op jit(solution)/shard_map/ppermute | solution.py:13
  14.5 4.9 %multiply_convert_fusion.2 = (f16[128,2048]{1,0:T(8,128)(2,1)S(1)}, f32[128,2048]{1,0:T(8,128)S(1)}) fusion(bf16[2048,2048]{1,0:T(8,128)(2,1)} %param.4, bf16[1,2,128,2048]{3,2,1,0:T(8,128)(2,1)S(1)} %bitcast.186, s32[]{:T(128)S(6)} %select_n.146, bf16[2048]{0:T(1024)(128)(2,1)S(1)} %fusion.110), kind=kOutput, calls=%fused_computation.33 | convolution fusion | flops 1075314688 | bytes 10489860 | tf_op jit(solution)/shard_map/dot_general | solution.py:97
  20.0 4.9 %fusion.40 = f32[128,2048]{1,0:T(8,128)S(1)} fusion(bf16[2048,2048]{1,0:T(8,128)(2,1)} %param.4, bf16[1,2,128,2048]{3,2,1,0:T(8,128)(2,1)S(1)} %bitcast.183, s32[]{:T(128)S(6)} %select_n.145, bf16[2048]{0:T(1024)(128)(2,1)S(1)} %fusion.111), kind=kOutput, calls=%fused_computation.95 | convolution fusion | flops 1074003968 | bytes 9965572 | tf_op jit(solution)/shard_map/dot_general | solution.py:101
  29.3 2.0 %collective-permute-start.5 = (f16[128,2048]{1,0:T(8,128)(2,1)S(1)}, f16[128,2048]{1,0:T(8,128)(2,1)S(1)}, u32[]{:S(2)}, u32[]{:S(2)}) collective-permute-start(f16[128,2048]{1,0:T(8,128)(2,1)S(1)} %get-tuple-element.68), channel_id=1, source_target_pairs={{0,4},{4,0},{8,12},{12,8},{16,20},{20,16},{24,28},{28,24},{1,5},{5... | collective-permute-start | bytes 1572872 | tf_op jit(solution)/shard_map/ppermute | solution.py:13
  31.3 3.6 %collective-permute-done.3 = f16[128,2048]{1,0:T(8,128)(2,1)S(1)} collective-permute-done((f16[128,2048]{1,0:T(8,128)(2,1)S(1)}, f16[128,2048]{1,0:T(8,128)(2,1)S(1)}, u32[]{:S(2)}, u32[]{:S(2)}) %collective-permute-start.3) | collective-permute-done | bytes 524320 | tf_op jit(solution)/shard_map/ppermute | solution.py:13
  35.6 1.6 %collective-permute-start.6 = (f16[2,128,512]{2,1,0:T(8,128)(2,1)S(1)}, f16[2,128,512]{2,1,0:T(8,128)(2,1)S(1)}, u32[]{:S(2)}, u32[]{:S(2)}) collective-permute-start(f16[2,128,512]{2,1,0:T(8,128)(2,1)S(1)} %multiply_convert_fusion.7), channel_id=1, source_target_pairs={{0,8},{4,12},{8,0},{12,4},{16,24},{20,28},{24,16},{28,20},{1,9},{5... | collective-permute-start | bytes 786440 | tf_op jit(solution)/shard_map/ppermute | solution.py:13
  40.5 1.6 %collective-permute-start.16 = (bf16[2,256,512]{2,1,0:T(8,128)(2,1)S(1)}, bf16[2,256,512]{2,1,0:T(8,128)(2,1)S(1)}, u32[]{:S(2)}, u32[]{:S(2)}) collective-permute-start(bf16[2,256,512]{2,1,0:T(8,128)(2,1)S(1)} %get-tuple-element.34), channel_id=1, source_target_pairs={{0,8},{4,12},{8,0},{12,4},{16,24},{20,28},{24,16},{28,20},{1,9},{5... | collective-permute-start | bytes 1572872 | tf_op jit(solution)/shard_map/ppermute | solution.py:13
  42.1 8.4 %collective-permute-done.8 = f16[2,128,512]{2,1,0:T(8,128)(2,1)S(1)} collective-permute-done((f16[2,128,512]{2,1,0:T(8,128)(2,1)S(1)}, f16[2,128,512]{2,1,0:T(8,128)(2,1)S(1)}, u32[]{:S(2)}, u32[]{:S(2)}) %collective-permute-start.8) | collective-permute-done | bytes 262176 | tf_op jit(solution)/shard_map/ppermute | solution.py:13
  50.7 2.7 %collective-permute-start.11 = (f16[1,128,512]{2,1,0:T(8,128)(2,1)S(1)}, f16[1,128,512]{2,1,0:T(8,128)(2,1)S(1)}, u32[]{:S(2)}, u32[]{:S(2)}) collective-permute-start(f16[1,128,512]{2,1,0:T(8,128)(2,1)S(1)} %multiply_convert_fusion.14), channel_id=1, source_target_pairs={{0,16},{4,20},{8,24},{12,28},{16,0},{20,4},{24,8},{28,12},{1,17},{... | collective-permute-start | bytes 393224 | tf_op jit(solution)/shard_map/ppermute | solution.py:13
  57.3 2.9 %collective-permute-start.12 = (f16[128,2048]{1,0:T(8,128)(2,1)S(1)}, f16[128,2048]{1,0:T(8,128)(2,1)S(1)}, u32[]{:S(2)}, u32[]{:S(2)}) collective-permute-start(f16[128,2048]{1,0:T(8,128)(2,1)S(1)} %get-tuple-element.62), channel_id=1, source_target_pairs={{0,4},{4,0},{8,12},{12,8},{16,20},{20,16},{24,28},{28,24},{1,5},{5... | collective-permute-start | bytes 1572872 | tf_op jit(solution)/shard_map/ppermute | solution.py:13
  60.2 5.4 %collective-permute-done.16 = bf16[2,256,512]{2,1,0:T(8,128)(2,1)S(1)} collective-permute-done((bf16[2,256,512]{2,1,0:T(8,128)(2,1)S(1)}, bf16[2,256,512]{2,1,0:T(8,128)(2,1)S(1)}, u32[]{:S(2)}, u32[]{:S(2)}) %collective-permute-start.16) | collective-permute-done | bytes 524320 | tf_op jit(solution)/shard_map/ppermute | solution.py:13
  67.2 1.9 %collective-permute-done.12 = f16[128,2048]{1,0:T(8,128)(2,1)S(1)} collective-permute-done((f16[128,2048]{1,0:T(8,128)(2,1)S(1)}, f16[128,2048]{1,0:T(8,128)(2,1)S(1)}, u32[]{:S(2)}, u32[]{:S(2)}) %collective-permute-start.12) | collective-permute-done | bytes 524320 | tf_op jit(solution)/shard_map/ppermute | solution.py:13
  69.6 3.6 %collective-permute-start.10 = (f16[2,128,512]{2,1,0:T(8,128)(2,1)S(1)}, f16[2,128,512]{2,1,0:T(8,128)(2,1)S(1)}, u32[]{:S(2)}, u32[]{:S(2)}) collective-permute-start(f16[2,128,512]{2,1,0:T(8,128)(2,1)S(1)} %multiply_convert_fusion.5), channel_id=1, source_target_pairs={{0,8},{4,12},{8,0},{12,4},{16,24},{20,28},{24,16},{28,20},{1,9},{5... | collective-permute-start | bytes 786440 | tf_op jit(solution)/shard_map/ppermute | solution.py:13
  73.6 6.6 %collective-permute-done.10 = f16[2,128,512]{2,1,0:T(8,128)(2,1)S(1)} collective-permute-done((f16[2,128,512]{2,1,0:T(8,128)(2,1)S(1)}, f16[2,128,512]{2,1,0:T(8,128)(2,1)S(1)}, u32[]{:S(2)}, u32[]{:S(2)}) %collective-permute-start.10) | collective-permute-done | bytes 262176 | tf_op jit(solution)/shard_map/ppermute | solution.py:13
  81.6 1.6 %collective-permute-done.13 = f16[2,128,512]{2,1,0:T(8,128)(2,1)S(1)} collective-permute-done((f16[2,128,512]{2,1,0:T(8,128)(2,1)S(1)}, f16[2,128,512]{2,1,0:T(8,128)(2,1)S(1)}, u32[]{:S(2)}, u32[]{:S(2)}) %collective-permute-start.13) | collective-permute-done | bytes 262176 | tf_op jit(solution)/shard_map/ppermute | solution.py:13
  84.8 2.9 %collective-permute-done.14 = f16[1,128,512]{2,1,0:T(8,128)(2,1)S(1)} collective-permute-done((f16[1,128,512]{2,1,0:T(8,128)(2,1)S(1)}, f16[1,128,512]{2,1,0:T(8,128)(2,1)S(1)}, u32[]{:S(2)}, u32[]{:S(2)}) %collective-permute-start.14) | collective-permute-done | bytes 131104 | tf_op jit(solution)/shard_map/ppermute | solution.py:13
  87.8 3.0 %collective-permute-done.15 = f16[1,128,512]{2,1,0:T(8,128)(2,1)S(1)} collective-permute-done((f16[1,128,512]{2,1,0:T(8,128)(2,1)S(1)}, f16[1,128,512]{2,1,0:T(8,128)(2,1)S(1)}, u32[]{:S(2)}, u32[]{:S(2)}) %collective-permute-start.15) | collective-permute-done | bytes 131104 | tf_op jit(solution)/shard_map/ppermute | solution.py:13
  95.6 2.0 %collective-permute-start.22 = (f16[128,512]{1,0:T(8,128)(2,1)S(1)}, f16[128,512]{1,0:T(8,128)(2,1)S(1)}, u32[]{:S(2)}, u32[]{:S(2)}) collective-permute-start(f16[128,512]{1,0:T(8,128)(2,1)S(1)} %multiply_convert_fusion.11), channel_id=1, source_target_pairs={{0,2},{1,3},{2,0},{3,1},{4,6},{5,7},{6,4},{7,5},{8,10},{9,11},{10,... | collective-permute-start | bytes 393224 | tf_op jit(solution)/shard_map/ppermute | solution.py:13
  98.1 9.7 %collective-permute-done.21 = f16[400,512]{1,0:T(8,128)(2,1)S(1)} collective-permute-done((f16[400,512]{1,0:T(8,128)(2,1)S(1)}, f16[400,512]{1,0:T(8,128)(2,1)S(1)}, u32[]{:S(2)}, u32[]{:S(2)}) %collective-permute-start.21) | collective-permute-done | bytes 409632 | tf_op jit(solution)/shard_map/ppermute | solution.py:13
  108.8 2.7 %collective-permute-start.24 = (f16[144,512]{1,0:T(8,128)(2,1)S(1)}, f16[144,512]{1,0:T(8,128)(2,1)S(1)}, u32[]{:S(2)}, u32[]{:S(2)}) collective-permute-start(f16[144,512]{1,0:T(8,128)(2,1)S(1)} %pad_maximum_fusion.10), channel_id=1, source_target_pairs={{0,16},{4,20},{8,24},{12,28},{16,0},{20,4},{24,8},{28,12},{1,17},{... | collective-permute-start | bytes 442376 | tf_op jit(solution)/shard_map/ppermute | solution.py:13
  111.5 1.6 %collective-permute-start.25 = (f16[144,512]{1,0:T(8,128)(2,1)S(1)}, f16[144,512]{1,0:T(8,128)(2,1)S(1)}, u32[]{:S(2)}, u32[]{:S(2)}) collective-permute-start(f16[144,512]{1,0:T(8,128)(2,1)S(1)} %pad_maximum_fusion.11), channel_id=1, source_target_pairs={{0,24},{4,28},{8,16},{12,20},{16,8},{20,12},{24,0},{28,4},{1,25},{... | collective-permute-start | bytes 442376 | tf_op jit(solution)/shard_map/ppermute | solution.py:13
  114.6 7.1 %collective-permute-done.24 = f16[144,512]{1,0:T(8,128)(2,1)S(1)} collective-permute-done((f16[144,512]{1,0:T(8,128)(2,1)S(1)}, f16[144,512]{1,0:T(8,128)(2,1)S(1)}, u32[]{:S(2)}, u32[]{:S(2)}) %collective-permute-start.24) | collective-permute-done | bytes 147488 | tf_op jit(solution)/shard_map/ppermute | solution.py:13
  (142 shorter events, 30.2 us)
Async XLA Ops:
  0.0 14.5 %collective-permute-start = (bf16[256,2048]{1,0:T(8,128)(2,1)}, bf16[256,2048]{1,0:T(8,128)(2,1)S(1)}, u32[]{:S(2)}, u32[]{:S(2)}) collective-permute-start(bf16[256,2048]{1,0:T(8,128)(2,1)} %param.3), channel_id=1, source_target_pairs={{0,1},{1,0},{2,3},{3,2},{4,5},{5,4},{6,7},{7,6},{8,9},{9,8},{10,11... | collective-permute-start | bytes 3145736 | tf_op jit(solution)/shard_map/ppermute | solution.py:13
  0.5 27.2 %collective-permute-start.2 = (bf16[256,2048]{1,0:T(8,128)(2,1)}, bf16[256,2048]{1,0:T(8,128)(2,1)S(1)}, u32[]{:S(2)}, u32[]{:S(2)}) collective-permute-start(bf16[256,2048]{1,0:T(8,128)(2,1)} %param.3), channel_id=1, source_target_pairs={{0,2},{1,3},{2,0},{3,1},{4,6},{5,7},{6,4},{7,5},{8,10},{9,11},{10,... | collective-permute-start | bytes 3145736 | tf_op jit(solution)/shard_map/ppermute | solution.py:13
  8.8 16.2 %collective-permute-start.1 = (f16[128,2048]{1,0:T(8,128)(2,1)}, f16[128,2048]{1,0:T(8,128)(2,1)}, u32[]{:S(2)}, u32[]{:S(2)}) collective-permute-start(f16[128,2048]{1,0:T(8,128)(2,1)} %get-tuple-element.66), channel_id=1, source_target_pairs={{0,4},{4,0},{8,12},{12,8},{16,20},{20,16},{24,28},{28,24},{1,5},{5... | collective-permute-start | bytes 1572872 | tf_op jit(solution)/shard_map/ppermute | solution.py:13
  11.7 27.5 %collective-permute-start.7 = (bf16[1,256,1024]{2,1,0:T(8,128)(2,1)S(1)}, bf16[1,256,1024]{2,1,0:T(8,128)(2,1)}, u32[]{:S(2)}, u32[]{:S(2)}) collective-permute-start(bf16[1,256,1024]{2,1,0:T(8,128)(2,1)S(1)} %get-tuple-element.36), channel_id=1, source_target_pairs={{0,16},{4,20},{8,24},{12,28},{16,0},{20,4},{24,8},{28,12},{1,17},{... | collective-permute-start | bytes 1572872 | tf_op jit(solution)/shard_map/ppermute | solution.py:13
  19.5 15.5 %collective-permute-start.3 = (f16[128,2048]{1,0:T(8,128)(2,1)S(1)}, f16[128,2048]{1,0:T(8,128)(2,1)S(1)}, u32[]{:S(2)}, u32[]{:S(2)}) collective-permute-start(f16[128,2048]{1,0:T(8,128)(2,1)S(1)} %get-tuple-element.64), channel_id=1, source_target_pairs={{0,4},{4,0},{8,12},{12,8},{16,20},{20,16},{24,28},{28,24},{1,5},{5... | collective-permute-start | bytes 1572872 | tf_op jit(solution)/shard_map/ppermute | solution.py:13
  29.3 27.2 %collective-permute-start.5 = (f16[128,2048]{1,0:T(8,128)(2,1)S(1)}, f16[128,2048]{1,0:T(8,128)(2,1)S(1)}, u32[]{:S(2)}, u32[]{:S(2)}) collective-permute-start(f16[128,2048]{1,0:T(8,128)(2,1)S(1)} %get-tuple-element.68), channel_id=1, source_target_pairs={{0,4},{4,0},{8,12},{12,8},{16,20},{20,16},{24,28},{28,24},{1,5},{5... | collective-permute-start | bytes 1572872 | tf_op jit(solution)/shard_map/ppermute | solution.py:13
  31.3 22.0 %collective-permute-start.4 = (bf16[256,2048]{1,0:T(8,128)(2,1)S(1)}, bf16[256,2048]{1,0:T(8,128)(2,1)S(1)}, u32[]{:S(2)}, u32[]{:S(2)}) collective-permute-start(bf16[256,2048]{1,0:T(8,128)(2,1)S(1)} %collective-permute-done.2), channel_id=1, source_target_pairs={{0,1},{1,0},{2,3},{3,2},{4,5},{5,4},{6,7},{7,6},{8,9},{9,8},{10,11... | collective-permute-start | bytes 3145736 | tf_op jit(solution)/shard_map/ppermute | solution.py:13
  35.6 21.1 %collective-permute-start.6 = (f16[2,128,512]{2,1,0:T(8,128)(2,1)S(1)}, f16[2,128,512]{2,1,0:T(8,128)(2,1)S(1)}, u32[]{:S(2)}, u32[]{:S(2)}) collective-permute-start(f16[2,128,512]{2,1,0:T(8,128)(2,1)S(1)} %multiply_convert_fusion.7), channel_id=1, source_target_pairs={{0,8},{4,12},{8,0},{12,4},{16,24},{20,28},{24,16},{28,20},{1,9},{5... | collective-permute-start | bytes 786440 | tf_op jit(solution)/shard_map/ppermute | solution.py:13
  37.3 13.2 %collective-permute-start.8 = (f16[2,128,512]{2,1,0:T(8,128)(2,1)S(1)}, f16[2,128,512]{2,1,0:T(8,128)(2,1)S(1)}, u32[]{:S(2)}, u32[]{:S(2)}) collective-permute-start(f16[2,128,512]{2,1,0:T(8,128)(2,1)S(1)} %multiply_convert_fusion.6), channel_id=1, source_target_pairs={{0,8},{4,12},{8,0},{12,4},{16,24},{20,28},{24,16},{28,20},{1,9},{5... | collective-permute-start | bytes 786440 | tf_op jit(solution)/shard_map/ppermute | solution.py:13
  40.5 25.1 %collective-permute-start.16 = (bf16[2,256,512]{2,1,0:T(8,128)(2,1)S(1)}, bf16[2,256,512]{2,1,0:T(8,128)(2,1)S(1)}, u32[]{:S(2)}, u32[]{:S(2)}) collective-permute-start(bf16[2,256,512]{2,1,0:T(8,128)(2,1)S(1)} %get-tuple-element.34), channel_id=1, source_target_pairs={{0,8},{4,12},{8,0},{12,4},{16,24},{20,28},{24,16},{28,20},{1,9},{5... | collective-permute-start | bytes 1572872 | tf_op jit(solution)/shard_map/ppermute | solution.py:13
  50.7 30.8 %collective-permute-start.11 = (f16[1,128,512]{2,1,0:T(8,128)(2,1)S(1)}, f16[1,128,512]{2,1,0:T(8,128)(2,1)S(1)}, u32[]{:S(2)}, u32[]{:S(2)}) collective-permute-start(f16[1,128,512]{2,1,0:T(8,128)(2,1)S(1)} %multiply_convert_fusion.14), channel_id=1, source_target_pairs={{0,16},{4,20},{8,24},{12,28},{16,0},{20,4},{24,8},{28,12},{1,17},{... | collective-permute-start | bytes 393224 | tf_op jit(solution)/shard_map/ppermute | solution.py:13
  56.9 16.4 %collective-permute-start.9 = (f16[1,128,512]{2,1,0:T(8,128)(2,1)S(1)}, f16[1,128,512]{2,1,0:T(8,128)(2,1)S(1)}, u32[]{:S(2)}, u32[]{:S(2)}) collective-permute-start(f16[1,128,512]{2,1,0:T(8,128)(2,1)S(1)} %multiply_convert_fusion.15), channel_id=1, source_target_pairs={{0,16},{4,20},{8,24},{12,28},{16,0},{20,4},{24,8},{28,12},{1,17},{... | collective-permute-start | bytes 393224 | tf_op jit(solution)/shard_map/ppermute | solution.py:13
  57.3 11.8 %collective-permute-start.12 = (f16[128,2048]{1,0:T(8,128)(2,1)S(1)}, f16[128,2048]{1,0:T(8,128)(2,1)S(1)}, u32[]{:S(2)}, u32[]{:S(2)}) collective-permute-start(f16[128,2048]{1,0:T(8,128)(2,1)S(1)} %get-tuple-element.62), channel_id=1, source_target_pairs={{0,4},{4,0},{8,12},{12,8},{16,20},{20,16},{24,28},{28,24},{1,5},{5... | collective-permute-start | bytes 1572872 | tf_op jit(solution)/shard_map/ppermute | solution.py:13
  65.7 25.4 %collective-permute-start.17 = (bf16[4,256,512]{2,1,0:T(8,128)(2,1)S(1)}, bf16[4,256,512]{2,1,0:T(8,128)(2,1)S(1)}, u32[]{:S(2)}, u32[]{:S(2)}) collective-permute-start(bf16[4,256,512]{2,1,0:T(8,128)(2,1)S(1)} %pad_maximum_fusion), channel_id=1, source_target_pairs={{0,4},{4,0},{8,12},{12,8},{16,20},{20,16},{24,28},{28,24},{1,5},{5... | collective-permute-start | bytes 3145736 | tf_op jit(solution)/shard_map/ppermute | solution.py:13
  69.6 10.6 %collective-permute-start.10 = (f16[2,128,512]{2,1,0:T(8,128)(2,1)S(1)}, f16[2,128,512]{2,1,0:T(8,128)(2,1)S(1)}, u32[]{:S(2)}, u32[]{:S(2)}) collective-permute-start(f16[2,128,512]{2,1,0:T(8,128)(2,1)S(1)} %multiply_convert_fusion.5), channel_id=1, source_target_pairs={{0,8},{4,12},{8,0},{12,4},{16,24},{20,28},{24,16},{28,20},{1,9},{5... | collective-permute-start | bytes 786440 | tf_op jit(solution)/shard_map/ppermute | solution.py:13
  73.5 9.8 %collective-permute-start.13 = (f16[2,128,512]{2,1,0:T(8,128)(2,1)S(1)}, f16[2,128,512]{2,1,0:T(8,128)(2,1)S(1)}, u32[]{:S(2)}, u32[]{:S(2)}) collective-permute-start(f16[2,128,512]{2,1,0:T(8,128)(2,1)S(1)} %multiply_convert_fusion.4), channel_id=1, source_target_pairs={{0,8},{4,12},{8,0},{12,4},{16,24},{20,28},{24,16},{28,20},{1,9},{5... | collective-permute-start | bytes 786440 | tf_op jit(solution)/shard_map/ppermute | solution.py:13
  80.4 7.3 %collective-permute-start.14 = (f16[1,128,512]{2,1,0:T(8,128)(2,1)S(1)}, f16[1,128,512]{2,1,0:T(8,128)(2,1)S(1)}, u32[]{:S(2)}, u32[]{:S(2)}) collective-permute-start(f16[1,128,512]{2,1,0:T(8,128)(2,1)S(1)} %multiply_convert_fusion.13), channel_id=1, source_target_pairs={{0,16},{4,20},{8,24},{12,28},{16,0},{20,4},{24,8},{28,12},{1,17},{... | collective-permute-start | bytes 393224 | tf_op jit(solution)/shard_map/ppermute | solution.py:13
  83.4 7.3 %collective-permute-start.15 = (f16[1,128,512]{2,1,0:T(8,128)(2,1)S(1)}, f16[1,128,512]{2,1,0:T(8,128)(2,1)S(1)}, u32[]{:S(2)}, u32[]{:S(2)}) collective-permute-start(f16[1,128,512]{2,1,0:T(8,128)(2,1)S(1)} %multiply_convert_fusion.12), channel_id=1, source_target_pairs={{0,16},{4,20},{8,24},{12,28},{16,0},{20,4},{24,8},{28,12},{1,17},{... | collective-permute-start | bytes 393224 | tf_op jit(solution)/shard_map/ppermute | solution.py:13
  93.2 4.4 %collective-permute-start.18 = (f32[4,128,512]{2,1,0:T(8,128)S(1)}, f32[4,128,512]{2,1,0:T(8,128)S(1)}, u32[]{:S(2)}, u32[]{:S(2)}) collective-permute-start(f32[4,128,512]{2,1,0:T(8,128)S(1)} %convolution_add_fusion.1), channel_id=1, source_target_pairs={{0,1},{1,0},{2,3},{3,2},{4,5},{5,4},{6,7},{7,6},{8,9},{9,8},{10,11... | collective-permute-start | bytes 3145736 | tf_op jit(solution)/shard_map/ppermute | solution.py:13
  95.4 12.4 %collective-permute-start.21 = (f16[400,512]{1,0:T(8,128)(2,1)S(1)}, f16[400,512]{1,0:T(8,128)(2,1)S(1)}, u32[]{:S(2)}, u32[]{:S(2)}) collective-permute-start(f16[400,512]{1,0:T(8,128)(2,1)S(1)} %pad_maximum_fusion.8), channel_id=1, source_target_pairs={{0,2},{1,3},{2,0},{3,1},{4,6},{5,7},{6,4},{7,5},{8,10},{9,11},{10,... | collective-permute-start | bytes 1228808 | tf_op jit(solution)/shard_map/ppermute | solution.py:13
  95.6 26.2 %collective-permute-start.22 = (f16[128,512]{1,0:T(8,128)(2,1)S(1)}, f16[128,512]{1,0:T(8,128)(2,1)S(1)}, u32[]{:S(2)}, u32[]{:S(2)}) collective-permute-start(f16[128,512]{1,0:T(8,128)(2,1)S(1)} %multiply_convert_fusion.11), channel_id=1, source_target_pairs={{0,2},{1,3},{2,0},{3,1},{4,6},{5,7},{6,4},{7,5},{8,10},{9,11},{10,... | collective-permute-start | bytes 393224 | tf_op jit(solution)/shard_map/ppermute | solution.py:13
  108.4 6.2 %collective-permute-start.23 = (f16[144,512]{1,0:T(8,128)(2,1)S(1)}, f16[144,512]{1,0:T(8,128)(2,1)S(1)}, u32[]{:S(2)}, u32[]{:S(2)}) collective-permute-start(f16[144,512]{1,0:T(8,128)(2,1)S(1)} %pad_maximum_fusion.9), channel_id=1, source_target_pairs={{0,8},{4,12},{8,0},{12,4},{16,24},{20,28},{24,16},{28,20},{1,9},{5... | collective-permute-start | bytes 442376 | tf_op jit(solution)/shard_map/ppermute | solution.py:13
  108.8 13.0 %collective-permute-start.24 = (f16[144,512]{1,0:T(8,128)(2,1)S(1)}, f16[144,512]{1,0:T(8,128)(2,1)S(1)}, u32[]{:S(2)}, u32[]{:S(2)}) collective-permute-start(f16[144,512]{1,0:T(8,128)(2,1)S(1)} %pad_maximum_fusion.10), channel_id=1, source_target_pairs={{0,16},{4,20},{8,24},{12,28},{16,0},{20,4},{24,8},{28,12},{1,17},{... | collective-permute-start | bytes 442376 | tf_op jit(solution)/shard_map/ppermute | solution.py:13
  111.5 10.2 %collective-permute-start.25 = (f16[144,512]{1,0:T(8,128)(2,1)S(1)}, f16[144,512]{1,0:T(8,128)(2,1)S(1)}, u32[]{:S(2)}, u32[]{:S(2)}) collective-permute-start(f16[144,512]{1,0:T(8,128)(2,1)S(1)} %pad_maximum_fusion.11), channel_id=1, source_target_pairs={{0,24},{4,28},{8,16},{12,20},{16,8},{20,12},{24,0},{28,4},{1,25},{... | collective-permute-start | bytes 442376 | tf_op jit(solution)/shard_map/ppermute | solution.py:13
  (5 other events, 24.4 us)

commit v4 on v3

--- a/solution.py
+++ b/solution.py
@@ -191,7 +191,7 @@
 
     def norm_rows(feature_sq, tgt_sq):
         rows = jnp.concatenate([jnp.pad(feature_sq, ((0, 0), (0, cols - own))), tgt_sq[None]])
-        return jnp.pad(rows, ((0, -rows.shape[0] % 16), (0, 0)))
+        return jnp.pad(rows, ((0, -rows.shape[0] % 8), (0, 0)))
 
     def coded(product, norms):
         return jnp.concatenate([encode(product, product_gain), encode(jnp.sqrt(norms), NORM_GAIN)])

time: 123 us -> 122 us (level)
  transfers between devices with their start and end apart: 26 -> 26, of which waited for: 12 -> 12; matrix products, arithmetic and copies ran while one was open for 27% -> 28% of each run, Pallas kernels for 0% -> 0%
where the time goes in v4:
time: 122 us
  waiting for transfers between devices  52.1 us (43%)
  starting transfers between devices  33.9 us (28%)
  matrix products  24.8 us (20%)
  other arithmetic  9.62 us (8%)
    ppermute x26, waiting for transfers between devices, swap(): return lax.ppermute(value, axis, [(i, i ^ bit) for i in range(size)])  52.1 us
    ppermute x26, starting transfers between devices, swap(): return lax.ppermute(value, axis, [(i, i ^ bit) for i in range(size)])  33.9 us
    dot_general x4, matrix products, partial_away(): jnp.dot(then(side(chunk, 1 - py)), proj_matrix, preferred_element_type=F32)  13.8 us
    dot_general x4, matrix products, partial_kept(): jnp.dot(then(side(chunk, py)), proj_matrix, preferred_element_type=F32)  9.08 us
  transfers between devices with their start and end apart: 26, of which 12 were waited for; matrix products, arithmetic and copies ran while one was open for 28% of the time, Pallas kernels for 0%

profile of v4, /device:TPU:0, one launch (start us, length us, event | category | flops | bytes accessed | tf_op | source)
XLA Modules:
  0.0 122.0 jit_solution(17423860202245963705)
XLA Ops:
  0.5 2.5 %collective-permute-start.2 = (bf16[256,2048]{1,0:T(8,128)(2,1)}, bf16[256,2048]{1,0:T(8,128)(2,1)S(1)}, u32[]{:S(2)}, u32[]{:S(2)}) collective-permute-start(bf16[256,2048]{1,0:T(8,128)(2,1)} %param.3), channel_id=1, source_target_pairs={{0,2},{1,3},{2,0},{3,1},{4,6},{5,7},{6,4},{7,5},{8,10},{9,11},{10,... | collective-permute-start | bytes 3145736 | tf_op jit(solution)/shard_map/ppermute | solution.py:13
  2.9 5.8 %multiply_convert_fusion.3 = (f16[128,2048]{1,0:T(8,128)(2,1)}, f32[128,2048]{1,0:T(8,128)S(1)}) fusion(bf16[2048,2048]{1,0:T(8,128)(2,1)} %param.4, bf16[1,2,128,2048]{3,2,1,0:T(8,128)(2,1)} %bitcast.182, s32[]{:T(128)S(6)} %select_n.146), kind=kOutput, calls=%fused_computation.34 | convolution fusion | flops 1075052544 | bytes 10485764 | tf_op jit(solution)/shard_map/dot_general | solution.py:97
  11.7 2.7 %collective-permute-start.7 = (bf16[1,256,1024]{2,1,0:T(8,128)(2,1)S(1)}, bf16[1,256,1024]{2,1,0:T(8,128)(2,1)}, u32[]{:S(2)}, u32[]{:S(2)}) collective-permute-start(bf16[1,256,1024]{2,1,0:T(8,128)(2,1)S(1)} %get-tuple-element.36), channel_id=1, source_target_pairs={{0,16},{4,20},{8,24},{12,28},{16,0},{20,4},{24,8},{28,12},{1,17},{... | collective-permute-start | bytes 1572872 | tf_op jit(solution)/shard_map/ppermute | solution.py:13
  14.5 4.9 %multiply_convert_fusion.2 = (f16[128,2048]{1,0:T(8,128)(2,1)S(1)}, f32[128,2048]{1,0:T(8,128)S(1)}) fusion(bf16[2048,2048]{1,0:T(8,128)(2,1)} %param.4, bf16[1,2,128,2048]{3,2,1,0:T(8,128)(2,1)S(1)} %bitcast.186, s32[]{:T(128)S(6)} %select_n.146, bf16[2048]{0:T(1024)(128)(2,1)S(1)} %fusion.110), kind=kOutput, calls=%fused_computation.33 | convolution fusion | flops 1075314688 | bytes 10489860 | tf_op jit(solution)/shard_map/dot_general | solution.py:97
  20.0 4.9 %fusion.40 = f32[128,2048]{1,0:T(8,128)S(1)} fusion(bf16[2048,2048]{1,0:T(8,128)(2,1)} %param.4, bf16[1,2,128,2048]{3,2,1,0:T(8,128)(2,1)S(1)} %bitcast.183, s32[]{:T(128)S(6)} %select_n.145, bf16[2048]{0:T(1024)(128)(2,1)S(1)} %fusion.111), kind=kOutput, calls=%fused_computation.95 | convolution fusion | flops 1074003968 | bytes 9965572 | tf_op jit(solution)/shard_map/dot_general | solution.py:101
  29.3 2.0 %collective-permute-start.5 = (f16[128,2048]{1,0:T(8,128)(2,1)S(1)}, f16[128,2048]{1,0:T(8,128)(2,1)S(1)}, u32[]{:S(2)}, u32[]{:S(2)}) collective-permute-start(f16[128,2048]{1,0:T(8,128)(2,1)S(1)} %get-tuple-element.68), channel_id=1, source_target_pairs={{0,4},{4,0},{8,12},{12,8},{16,20},{20,16},{24,28},{28,24},{1,5},{5... | collective-permute-start | bytes 1572872 | tf_op jit(solution)/shard_map/ppermute | solution.py:13
  31.3 3.6 %collective-permute-done.3 = f16[128,2048]{1,0:T(8,128)(2,1)S(1)} collective-permute-done((f16[128,2048]{1,0:T(8,128)(2,1)S(1)}, f16[128,2048]{1,0:T(8,128)(2,1)S(1)}, u32[]{:S(2)}, u32[]{:S(2)}) %collective-permute-start.3) | collective-permute-done | bytes 524320 | tf_op jit(solution)/shard_map/ppermute | solution.py:13
  35.6 1.6 %collective-permute-start.6 = (f16[2,128,512]{2,1,0:T(8,128)(2,1)S(1)}, f16[2,128,512]{2,1,0:T(8,128)(2,1)S(1)}, u32[]{:S(2)}, u32[]{:S(2)}) collective-permute-start(f16[2,128,512]{2,1,0:T(8,128)(2,1)S(1)} %multiply_convert_fusion.7), channel_id=1, source_target_pairs={{0,8},{4,12},{8,0},{12,4},{16,24},{20,28},{24,16},{28,20},{1,9},{5... | collective-permute-start | bytes 786440 | tf_op jit(solution)/shard_map/ppermute | solution.py:13
  40.5 1.6 %collective-permute-start.16 = (bf16[2,256,512]{2,1,0:T(8,128)(2,1)S(1)}, bf16[2,256,512]{2,1,0:T(8,128)(2,1)S(1)}, u32[]{:S(2)}, u32[]{:S(2)}) collective-permute-start(bf16[2,256,512]{2,1,0:T(8,128)(2,1)S(1)} %get-tuple-element.34), channel_id=1, source_target_pairs={{0,8},{4,12},{8,0},{12,4},{16,24},{20,28},{24,16},{28,20},{1,9},{5... | collective-permute-start | bytes 1572872 | tf_op jit(solution)/shard_map/ppermute | solution.py:13
  42.1 8.4 %collective-permute-done.8 = f16[2,128,512]{2,1,0:T(8,128)(2,1)S(1)} collective-permute-done((f16[2,128,512]{2,1,0:T(8,128)(2,1)S(1)}, f16[2,128,512]{2,1,0:T(8,128)(2,1)S(1)}, u32[]{:S(2)}, u32[]{:S(2)}) %collective-permute-start.8) | collective-permute-done | bytes 262176 | tf_op jit(solution)/shard_map/ppermute | solution.py:13
  50.7 2.7 %collective-permute-start.11 = (f16[1,128,512]{2,1,0:T(8,128)(2,1)S(1)}, f16[1,128,512]{2,1,0:T(8,128)(2,1)S(1)}, u32[]{:S(2)}, u32[]{:S(2)}) collective-permute-start(f16[1,128,512]{2,1,0:T(8,128)(2,1)S(1)} %multiply_convert_fusion.14), channel_id=1, source_target_pairs={{0,16},{4,20},{8,24},{12,28},{16,0},{20,4},{24,8},{28,12},{1,17},{... | collective-permute-start | bytes 393224 | tf_op jit(solution)/shard_map/ppermute | solution.py:13
  57.3 2.9 %collective-permute-start.12 = (f16[128,2048]{1,0:T(8,128)(2,1)S(1)}, f16[128,2048]{1,0:T(8,128)(2,1)S(1)}, u32[]{:S(2)}, u32[]{:S(2)}) collective-permute-start(f16[128,2048]{1,0:T(8,128)(2,1)S(1)} %get-tuple-element.62), channel_id=1, source_target_pairs={{0,4},{4,0},{8,12},{12,8},{16,20},{20,16},{24,28},{28,24},{1,5},{5... | collective-permute-start | bytes 1572872 | tf_op jit(solution)/shard_map/ppermute | solution.py:13
  60.2 5.4 %collective-permute-done.16 = bf16[2,256,512]{2,1,0:T(8,128)(2,1)S(1)} collective-permute-done((bf16[2,256,512]{2,1,0:T(8,128)(2,1)S(1)}, bf16[2,256,512]{2,1,0:T(8,128)(2,1)S(1)}, u32[]{:S(2)}, u32[]{:S(2)}) %collective-permute-start.16) | collective-permute-done | bytes 524320 | tf_op jit(solution)/shard_map/ppermute | solution.py:13
  67.2 1.9 %collective-permute-done.12 = f16[128,2048]{1,0:T(8,128)(2,1)S(1)} collective-permute-done((f16[128,2048]{1,0:T(8,128)(2,1)S(1)}, f16[128,2048]{1,0:T(8,128)(2,1)S(1)}, u32[]{:S(2)}, u32[]{:S(2)}) %collective-permute-start.12) | collective-permute-done | bytes 524320 | tf_op jit(solution)/shard_map/ppermute | solution.py:13
  69.6 3.6 %collective-permute-start.10 = (f16[2,128,512]{2,1,0:T(8,128)(2,1)S(1)}, f16[2,128,512]{2,1,0:T(8,128)(2,1)S(1)}, u32[]{:S(2)}, u32[]{:S(2)}) collective-permute-start(f16[2,128,512]{2,1,0:T(8,128)(2,1)S(1)} %multiply_convert_fusion.5), channel_id=1, source_target_pairs={{0,8},{4,12},{8,0},{12,4},{16,24},{20,28},{24,16},{28,20},{1,9},{5... | collective-permute-start | bytes 786440 | tf_op jit(solution)/shard_map/ppermute | solution.py:13
  73.6 6.6 %collective-permute-done.10 = f16[2,128,512]{2,1,0:T(8,128)(2,1)S(1)} collective-permute-done((f16[2,128,512]{2,1,0:T(8,128)(2,1)S(1)}, f16[2,128,512]{2,1,0:T(8,128)(2,1)S(1)}, u32[]{:S(2)}, u32[]{:S(2)}) %collective-permute-start.10) | collective-permute-done | bytes 262176 | tf_op jit(solution)/shard_map/ppermute | solution.py:13
  81.6 1.6 %collective-permute-done.13 = f16[2,128,512]{2,1,0:T(8,128)(2,1)S(1)} collective-permute-done((f16[2,128,512]{2,1,0:T(8,128)(2,1)S(1)}, f16[2,128,512]{2,1,0:T(8,128)(2,1)S(1)}, u32[]{:S(2)}, u32[]{:S(2)}) %collective-permute-start.13) | collective-permute-done | bytes 262176 | tf_op jit(solution)/shard_map/ppermute | solution.py:13
  84.8 2.9 %collective-permute-done.14 = f16[1,128,512]{2,1,0:T(8,128)(2,1)S(1)} collective-permute-done((f16[1,128,512]{2,1,0:T(8,128)(2,1)S(1)}, f16[1,128,512]{2,1,0:T(8,128)(2,1)S(1)}, u32[]{:S(2)}, u32[]{:S(2)}) %collective-permute-start.14) | collective-permute-done | bytes 131104 | tf_op jit(solution)/shard_map/ppermute | solution.py:13
  87.8 3.0 %collective-permute-done.15 = f16[1,128,512]{2,1,0:T(8,128)(2,1)S(1)} collective-permute-done((f16[1,128,512]{2,1,0:T(8,128)(2,1)S(1)}, f16[1,128,512]{2,1,0:T(8,128)(2,1)S(1)}, u32[]{:S(2)}, u32[]{:S(2)}) %collective-permute-start.15) | collective-permute-done | bytes 131104 | tf_op jit(solution)/shard_map/ppermute | solution.py:13
  95.6 2.0 %collective-permute-start.22 = (f16[128,512]{1,0:T(8,128)(2,1)S(1)}, f16[128,512]{1,0:T(8,128)(2,1)S(1)}, u32[]{:S(2)}, u32[]{:S(2)}) collective-permute-start(f16[128,512]{1,0:T(8,128)(2,1)S(1)} %multiply_convert_fusion.11), channel_id=1, source_target_pairs={{0,2},{1,3},{2,0},{3,1},{4,6},{5,7},{6,4},{7,5},{8,10},{9,11},{10,... | collective-permute-start | bytes 393224 | tf_op jit(solution)/shard_map/ppermute | solution.py:13
  98.1 9.5 %collective-permute-done.21 = f16[392,512]{1,0:T(8,128)(2,1)S(1)} collective-permute-done((f16[392,512]{1,0:T(8,128)(2,1)S(1)}, f16[392,512]{1,0:T(8,128)(2,1)S(1)}, u32[]{:S(2)}, u32[]{:S(2)}) %collective-permute-start.21) | collective-permute-done | bytes 401440 | tf_op jit(solution)/shard_map/ppermute | solution.py:13
  108.6 2.7 %collective-permute-start.24 = (f16[136,512]{1,0:T(8,128)(2,1)S(1)}, f16[136,512]{1,0:T(8,128)(2,1)S(1)}, u32[]{:S(2)}, u32[]{:S(2)}) collective-permute-start(f16[136,512]{1,0:T(8,128)(2,1)S(1)} %pad_maximum_fusion.10), channel_id=1, source_target_pairs={{0,16},{4,20},{8,24},{12,28},{16,0},{20,4},{24,8},{28,12},{1,17},{... | collective-permute-start | bytes 417800 | tf_op jit(solution)/shard_map/ppermute | solution.py:13
  111.3 1.6 %collective-permute-start.25 = (f16[136,512]{1,0:T(8,128)(2,1)S(1)}, f16[136,512]{1,0:T(8,128)(2,1)S(1)}, u32[]{:S(2)}, u32[]{:S(2)}) collective-permute-start(f16[136,512]{1,0:T(8,128)(2,1)S(1)} %pad_maximum_fusion.11), channel_id=1, source_target_pairs={{0,24},{4,28},{8,16},{12,20},{16,8},{20,12},{24,0},{28,4},{1,25},{... | collective-permute-start | bytes 417800 | tf_op jit(solution)/shard_map/ppermute | solution.py:13
  114.1 6.8 %collective-permute-done.24 = f16[136,512]{1,0:T(8,128)(2,1)S(1)} collective-permute-done((f16[136,512]{1,0:T(8,128)(2,1)S(1)}, f16[136,512]{1,0:T(8,128)(2,1)S(1)}, u32[]{:S(2)}, u32[]{:S(2)}) %collective-permute-start.24) | collective-permute-done | bytes 139296 | tf_op jit(solution)/shard_map/ppermute | solution.py:13
  (142 shorter events, 29.8 us)
Async XLA Ops:
  0.0 14.5 %collective-permute-start = (bf16[256,2048]{1,0:T(8,128)(2,1)}, bf16[256,2048]{1,0:T(8,128)(2,1)S(1)}, u32[]{:S(2)}, u32[]{:S(2)}) collective-permute-start(bf16[256,2048]{1,0:T(8,128)(2,1)} %param.3), channel_id=1, source_target_pairs={{0,1},{1,0},{2,3},{3,2},{4,5},{5,4},{6,7},{7,6},{8,9},{9,8},{10,11... | collective-permute-start | bytes 3145736 | tf_op jit(solution)/shard_map/ppermute | solution.py:13
  0.5 27.2 %collective-permute-start.2 = (bf16[256,2048]{1,0:T(8,128)(2,1)}, bf16[256,2048]{1,0:T(8,128)(2,1)S(1)}, u32[]{:S(2)}, u32[]{:S(2)}) collective-permute-start(bf16[256,2048]{1,0:T(8,128)(2,1)} %param.3), channel_id=1, source_target_pairs={{0,2},{1,3},{2,0},{3,1},{4,6},{5,7},{6,4},{7,5},{8,10},{9,11},{10,... | collective-permute-start | bytes 3145736 | tf_op jit(solution)/shard_map/ppermute | solution.py:13
  8.8 16.2 %collective-permute-start.1 = (f16[128,2048]{1,0:T(8,128)(2,1)}, f16[128,2048]{1,0:T(8,128)(2,1)}, u32[]{:S(2)}, u32[]{:S(2)}) collective-permute-start(f16[128,2048]{1,0:T(8,128)(2,1)} %get-tuple-element.66), channel_id=1, source_target_pairs={{0,4},{4,0},{8,12},{12,8},{16,20},{20,16},{24,28},{28,24},{1,5},{5... | collective-permute-start | bytes 1572872 | tf_op jit(solution)/shard_map/ppermute | solution.py:13
  11.7 27.5 %collective-permute-start.7 = (bf16[1,256,1024]{2,1,0:T(8,128)(2,1)S(1)}, bf16[1,256,1024]{2,1,0:T(8,128)(2,1)}, u32[]{:S(2)}, u32[]{:S(2)}) collective-permute-start(bf16[1,256,1024]{2,1,0:T(8,128)(2,1)S(1)} %get-tuple-element.36), channel_id=1, source_target_pairs={{0,16},{4,20},{8,24},{12,28},{16,0},{20,4},{24,8},{28,12},{1,17},{... | collective-permute-start | bytes 1572872 | tf_op jit(solution)/shard_map/ppermute | solution.py:13
  19.5 15.5 %collective-permute-start.3 = (f16[128,2048]{1,0:T(8,128)(2,1)S(1)}, f16[128,2048]{1,0:T(8,128)(2,1)S(1)}, u32[]{:S(2)}, u32[]{:S(2)}) collective-permute-start(f16[128,2048]{1,0:T(8,128)(2,1)S(1)} %get-tuple-element.64), channel_id=1, source_target_pairs={{0,4},{4,0},{8,12},{12,8},{16,20},{20,16},{24,28},{28,24},{1,5},{5... | collective-permute-start | bytes 1572872 | tf_op jit(solution)/shard_map/ppermute | solution.py:13
  29.3 27.2 %collective-permute-start.5 = (f16[128,2048]{1,0:T(8,128)(2,1)S(1)}, f16[128,2048]{1,0:T(8,128)(2,1)S(1)}, u32[]{:S(2)}, u32[]{:S(2)}) collective-permute-start(f16[128,2048]{1,0:T(8,128)(2,1)S(1)} %get-tuple-element.68), channel_id=1, source_target_pairs={{0,4},{4,0},{8,12},{12,8},{16,20},{20,16},{24,28},{28,24},{1,5},{5... | collective-permute-start | bytes 1572872 | tf_op jit(solution)/shard_map/ppermute | solution.py:13
  31.3 22.0 %collective-permute-start.4 = (bf16[256,2048]{1,0:T(8,128)(2,1)S(1)}, bf16[256,2048]{1,0:T(8,128)(2,1)S(1)}, u32[]{:S(2)}, u32[]{:S(2)}) collective-permute-start(bf16[256,2048]{1,0:T(8,128)(2,1)S(1)} %collective-permute-done.2), channel_id=1, source_target_pairs={{0,1},{1,0},{2,3},{3,2},{4,5},{5,4},{6,7},{7,6},{8,9},{9,8},{10,11... | collective-permute-start | bytes 3145736 | tf_op jit(solution)/shard_map/ppermute | solution.py:13
  35.6 21.1 %collective-permute-start.6 = (f16[2,128,512]{2,1,0:T(8,128)(2,1)S(1)}, f16[2,128,512]{2,1,0:T(8,128)(2,1)S(1)}, u32[]{:S(2)}, u32[]{:S(2)}) collective-permute-start(f16[2,128,512]{2,1,0:T(8,128)(2,1)S(1)} %multiply_convert_fusion.7), channel_id=1, source_target_pairs={{0,8},{4,12},{8,0},{12,4},{16,24},{20,28},{24,16},{28,20},{1,9},{5... | collective-permute-start | bytes 786440 | tf_op jit(solution)/shard_map/ppermute | solution.py:13
  37.3 13.2 %collective-permute-start.8 = (f16[2,128,512]{2,1,0:T(8,128)(2,1)S(1)}, f16[2,128,512]{2,1,0:T(8,128)(2,1)S(1)}, u32[]{:S(2)}, u32[]{:S(2)}) collective-permute-start(f16[2,128,512]{2,1,0:T(8,128)(2,1)S(1)} %multiply_convert_fusion.6), channel_id=1, source_target_pairs={{0,8},{4,12},{8,0},{12,4},{16,24},{20,28},{24,16},{28,20},{1,9},{5... | collective-permute-start | bytes 786440 | tf_op jit(solution)/shard_map/ppermute | solution.py:13
  40.5 25.1 %collective-permute-start.16 = (bf16[2,256,512]{2,1,0:T(8,128)(2,1)S(1)}, bf16[2,256,512]{2,1,0:T(8,128)(2,1)S(1)}, u32[]{:S(2)}, u32[]{:S(2)}) collective-permute-start(bf16[2,256,512]{2,1,0:T(8,128)(2,1)S(1)} %get-tuple-element.34), channel_id=1, source_target_pairs={{0,8},{4,12},{8,0},{12,4},{16,24},{20,28},{24,16},{28,20},{1,9},{5... | collective-permute-start | bytes 1572872 | tf_op jit(solution)/shard_map/ppermute | solution.py:13
  50.7 30.8 %collective-permute-start.11 = (f16[1,128,512]{2,1,0:T(8,128)(2,1)S(1)}, f16[1,128,512]{2,1,0:T(8,128)(2,1)S(1)}, u32[]{:S(2)}, u32[]{:S(2)}) collective-permute-start(f16[1,128,512]{2,1,0:T(8,128)(2,1)S(1)} %multiply_convert_fusion.14), channel_id=1, source_target_pairs={{0,16},{4,20},{8,24},{12,28},{16,0},{20,4},{24,8},{28,12},{1,17},{... | collective-permute-start | bytes 393224 | tf_op jit(solution)/shard_map/ppermute | solution.py:13
  56.9 16.4 %collective-permute-start.9 = (f16[1,128,512]{2,1,0:T(8,128)(2,1)S(1)}, f16[1,128,512]{2,1,0:T(8,128)(2,1)S(1)}, u32[]{:S(2)}, u32[]{:S(2)}) collective-permute-start(f16[1,128,512]{2,1,0:T(8,128)(2,1)S(1)} %multiply_convert_fusion.15), channel_id=1, source_target_pairs={{0,16},{4,20},{8,24},{12,28},{16,0},{20,4},{24,8},{28,12},{1,17},{... | collective-permute-start | bytes 393224 | tf_op jit(solution)/shard_map/ppermute | solution.py:13
  57.3 11.8 %collective-permute-start.12 = (f16[128,2048]{1,0:T(8,128)(2,1)S(1)}, f16[128,2048]{1,0:T(8,128)(2,1)S(1)}, u32[]{:S(2)}, u32[]{:S(2)}) collective-permute-start(f16[128,2048]{1,0:T(8,128)(2,1)S(1)} %get-tuple-element.62), channel_id=1, source_target_pairs={{0,4},{4,0},{8,12},{12,8},{16,20},{20,16},{24,28},{28,24},{1,5},{5... | collective-permute-start | bytes 1572872 | tf_op jit(solution)/shard_map/ppermute | solution.py:13
  65.7 25.4 %collective-permute-start.17 = (bf16[4,256,512]{2,1,0:T(8,128)(2,1)S(1)}, bf16[4,256,512]{2,1,0:T(8,128)(2,1)S(1)}, u32[]{:S(2)}, u32[]{:S(2)}) collective-permute-start(bf16[4,256,512]{2,1,0:T(8,128)(2,1)S(1)} %pad_maximum_fusion), channel_id=1, source_target_pairs={{0,4},{4,0},{8,12},{12,8},{16,20},{20,16},{24,28},{28,24},{1,5},{5... | collective-permute-start | bytes 3145736 | tf_op jit(solution)/shard_map/ppermute | solution.py:13
  69.6 10.6 %collective-permute-start.10 = (f16[2,128,512]{2,1,0:T(8,128)(2,1)S(1)}, f16[2,128,512]{2,1,0:T(8,128)(2,1)S(1)}, u32[]{:S(2)}, u32[]{:S(2)}) collective-permute-start(f16[2,128,512]{2,1,0:T(8,128)(2,1)S(1)} %multiply_convert_fusion.5), channel_id=1, source_target_pairs={{0,8},{4,12},{8,0},{12,4},{16,24},{20,28},{24,16},{28,20},{1,9},{5... | collective-permute-start | bytes 786440 | tf_op jit(solution)/shard_map/ppermute | solution.py:13
  73.5 9.8 %collective-permute-start.13 = (f16[2,128,512]{2,1,0:T(8,128)(2,1)S(1)}, f16[2,128,512]{2,1,0:T(8,128)(2,1)S(1)}, u32[]{:S(2)}, u32[]{:S(2)}) collective-permute-start(f16[2,128,512]{2,1,0:T(8,128)(2,1)S(1)} %multiply_convert_fusion.4), channel_id=1, source_target_pairs={{0,8},{4,12},{8,0},{12,4},{16,24},{20,28},{24,16},{28,20},{1,9},{5... | collective-permute-start | bytes 786440 | tf_op jit(solution)/shard_map/ppermute | solution.py:13
  80.4 7.3 %collective-permute-start.14 = (f16[1,128,512]{2,1,0:T(8,128)(2,1)S(1)}, f16[1,128,512]{2,1,0:T(8,128)(2,1)S(1)}, u32[]{:S(2)}, u32[]{:S(2)}) collective-permute-start(f16[1,128,512]{2,1,0:T(8,128)(2,1)S(1)} %multiply_convert_fusion.13), channel_id=1, source_target_pairs={{0,16},{4,20},{8,24},{12,28},{16,0},{20,4},{24,8},{28,12},{1,17},{... | collective-permute-start | bytes 393224 | tf_op jit(solution)/shard_map/ppermute | solution.py:13
  83.4 7.3 %collective-permute-start.15 = (f16[1,128,512]{2,1,0:T(8,128)(2,1)S(1)}, f16[1,128,512]{2,1,0:T(8,128)(2,1)S(1)}, u32[]{:S(2)}, u32[]{:S(2)}) collective-permute-start(f16[1,128,512]{2,1,0:T(8,128)(2,1)S(1)} %multiply_convert_fusion.12), channel_id=1, source_target_pairs={{0,16},{4,20},{8,24},{12,28},{16,0},{20,4},{24,8},{28,12},{1,17},{... | collective-permute-start | bytes 393224 | tf_op jit(solution)/shard_map/ppermute | solution.py:13
  93.2 4.4 %collective-permute-start.18 = (f32[4,128,512]{2,1,0:T(8,128)S(1)}, f32[4,128,512]{2,1,0:T(8,128)S(1)}, u32[]{:S(2)}, u32[]{:S(2)}) collective-permute-start(f32[4,128,512]{2,1,0:T(8,128)S(1)} %convolution_add_fusion.1), channel_id=1, source_target_pairs={{0,1},{1,0},{2,3},{3,2},{4,5},{5,4},{6,7},{7,6},{8,9},{9,8},{10,11... | collective-permute-start | bytes 3145736 | tf_op jit(solution)/shard_map/ppermute | solution.py:13
  95.4 12.2 %collective-permute-start.21 = (f16[392,512]{1,0:T(8,128)(2,1)S(1)}, f16[392,512]{1,0:T(8,128)(2,1)S(1)}, u32[]{:S(2)}, u32[]{:S(2)}) collective-permute-start(f16[392,512]{1,0:T(8,128)(2,1)S(1)} %pad_maximum_fusion.8), channel_id=1, source_target_pairs={{0,2},{1,3},{2,0},{3,1},{4,6},{5,7},{6,4},{7,5},{8,10},{9,11},{10,... | collective-permute-start | bytes 1204232 | tf_op jit(solution)/shard_map/ppermute | solution.py:13
  95.6 25.4 %collective-permute-start.22 = (f16[128,512]{1,0:T(8,128)(2,1)S(1)}, f16[128,512]{1,0:T(8,128)(2,1)S(1)}, u32[]{:S(2)}, u32[]{:S(2)}) collective-permute-start(f16[128,512]{1,0:T(8,128)(2,1)S(1)} %multiply_convert_fusion.11), channel_id=1, source_target_pairs={{0,2},{1,3},{2,0},{3,1},{4,6},{5,7},{6,4},{7,5},{8,10},{9,11},{10,... | collective-permute-start | bytes 393224 | tf_op jit(solution)/shard_map/ppermute | solution.py:13
  108.2 5.9 %collective-permute-start.23 = (f16[136,512]{1,0:T(8,128)(2,1)S(1)}, f16[136,512]{1,0:T(8,128)(2,1)S(1)}, u32[]{:S(2)}, u32[]{:S(2)}) collective-permute-start(f16[136,512]{1,0:T(8,128)(2,1)S(1)} %pad_maximum_fusion.9), channel_id=1, source_target_pairs={{0,8},{4,12},{8,0},{12,4},{16,24},{20,28},{24,16},{28,20},{1,9},{5... | collective-permute-start | bytes 417800 | tf_op jit(solution)/shard_map/ppermute | solution.py:13
  108.6 12.4 %collective-permute-start.24 = (f16[136,512]{1,0:T(8,128)(2,1)S(1)}, f16[136,512]{1,0:T(8,128)(2,1)S(1)}, u32[]{:S(2)}, u32[]{:S(2)}) collective-permute-start(f16[136,512]{1,0:T(8,128)(2,1)S(1)} %pad_maximum_fusion.10), channel_id=1, source_target_pairs={{0,16},{4,20},{8,24},{12,28},{16,0},{20,4},{24,8},{28,12},{1,17},{... | collective-permute-start | bytes 417800 | tf_op jit(solution)/shard_map/ppermute | solution.py:13
  111.3 9.6 %collective-permute-start.25 = (f16[136,512]{1,0:T(8,128)(2,1)S(1)}, f16[136,512]{1,0:T(8,128)(2,1)S(1)}, u32[]{:S(2)}, u32[]{:S(2)}) collective-permute-start(f16[136,512]{1,0:T(8,128)(2,1)S(1)} %pad_maximum_fusion.11), channel_id=1, source_target_pairs={{0,24},{4,28},{8,16},{12,20},{16,8},{20,12},{24,0},{28,4},{1,25},{... | collective-permute-start | bytes 417800 | tf_op jit(solution)/shard_map/ppermute | solution.py:13
  (5 other events, 24.4 us)

commit v5 on v4

--- a/solution.py
+++ b/solution.py
@@ -209,7 +209,7 @@
     tgt_sq = tgt_sq[0] + got_norms[n_z]
 
     norms = [norm_rows(feature_sq[k : k + 1], tgt_sq) for k in range(n_z)]
-    sends = [swap(coded(part[k - 1], norms[k]), "proj", n_p, 2 * k) for k in range(1, n_z)]
+    sends = [swap(coded(part[k - 1], norms[k]), "proj", n_p, 2 * k) for k in range(n_z - 1, 0, -1)]
     total = then(own_part[near])[0] + decode(codes[1], product_gain)
     norms = norms[0]
     for code in sends:

time: 122 us -> 123 us (level)
  transfers between devices with their start and end apart: 26 -> 26, of which waited for: 12 -> 12; matrix products, arithmetic and copies ran while one was open for 28% -> 27% of each run, Pallas kernels for 0% -> 0%
where the time goes in v5:
time: 123 us
  waiting for transfers between devices  52.8 us (43%)
  starting transfers between devices  33.9 us (28%)
  matrix products  24.8 us (20%)
  other arithmetic  9.63 us (8%)
    ppermute x26, waiting for transfers between devices, swap(): return lax.ppermute(value, axis, [(i, i ^ bit) for i in range(size)])  52.8 us
    ppermute x26, starting transfers between devices, swap(): return lax.ppermute(value, axis, [(i, i ^ bit) for i in range(size)])  33.9 us
    dot_general x4, matrix products, partial_away(): jnp.dot(then(side(chunk, 1 - py)), proj_matrix, preferred_element_type=F32)  13.8 us
    dot_general x4, matrix products, partial_kept(): jnp.dot(then(side(chunk, py)), proj_matrix, preferred_element_type=F32)  9.08 us
  transfers between devices with their start and end apart: 26, of which 12 were waited for; matrix products, arithmetic and copies ran while one was open for 27% of the time, Pallas kernels for 0%

profile of v5, /device:TPU:0, one launch (start us, length us, event | category | flops | bytes accessed | tf_op | source)
XLA Modules:
  0.0 122.7 jit_solution(1193649621964000004)
XLA Ops:
  0.5 2.5 %collective-permute-start.2 = (bf16[256,2048]{1,0:T(8,128)(2,1)}, bf16[256,2048]{1,0:T(8,128)(2,1)S(1)}, u32[]{:S(2)}, u32[]{:S(2)}) collective-permute-start(bf16[256,2048]{1,0:T(8,128)(2,1)} %param.3), channel_id=1, source_target_pairs={{0,2},{1,3},{2,0},{3,1},{4,6},{5,7},{6,4},{7,5},{8,10},{9,11},{10,... | collective-permute-start | bytes 3145736 | tf_op jit(solution)/shard_map/ppermute | solution.py:13
  2.9 5.8 %multiply_convert_fusion.3 = (f16[128,2048]{1,0:T(8,128)(2,1)}, f32[128,2048]{1,0:T(8,128)S(1)}) fusion(bf16[2048,2048]{1,0:T(8,128)(2,1)} %param.4, bf16[1,2,128,2048]{3,2,1,0:T(8,128)(2,1)} %bitcast.182, s32[]{:T(128)S(6)} %select_n.146), kind=kOutput, calls=%fused_computation.34 | convolution fusion | flops 1075052544 | bytes 10485764 | tf_op jit(solution)/shard_map/dot_general | solution.py:97
  11.7 2.7 %collective-permute-start.7 = (bf16[1,256,1024]{2,1,0:T(8,128)(2,1)S(1)}, bf16[1,256,1024]{2,1,0:T(8,128)(2,1)}, u32[]{:S(2)}, u32[]{:S(2)}) collective-permute-start(bf16[1,256,1024]{2,1,0:T(8,128)(2,1)S(1)} %get-tuple-element.36), channel_id=1, source_target_pairs={{0,16},{4,20},{8,24},{12,28},{16,0},{20,4},{24,8},{28,12},{1,17},{... | collective-permute-start | bytes 1572872 | tf_op jit(solution)/shard_map/ppermute | solution.py:13
  14.5 4.9 %multiply_convert_fusion.2 = (f16[128,2048]{1,0:T(8,128)(2,1)S(1)}, f32[128,2048]{1,0:T(8,128)S(1)}) fusion(bf16[2048,2048]{1,0:T(8,128)(2,1)} %param.4, bf16[1,2,128,2048]{3,2,1,0:T(8,128)(2,1)S(1)} %bitcast.186, s32[]{:T(128)S(6)} %select_n.146, bf16[2048]{0:T(1024)(128)(2,1)S(1)} %fusion.110), kind=kOutput, calls=%fused_computation.33 | convolution fusion | flops 1075314688 | bytes 10489860 | tf_op jit(solution)/shard_map/dot_general | solution.py:97
  20.0 4.9 %fusion.40 = f32[128,2048]{1,0:T(8,128)S(1)} fusion(bf16[2048,2048]{1,0:T(8,128)(2,1)} %param.4, bf16[1,2,128,2048]{3,2,1,0:T(8,128)(2,1)S(1)} %bitcast.183, s32[]{:T(128)S(6)} %select_n.145, bf16[2048]{0:T(1024)(128)(2,1)S(1)} %fusion.111), kind=kOutput, calls=%fused_computation.95 | convolution fusion | flops 1074003968 | bytes 9965572 | tf_op jit(solution)/shard_map/dot_general | solution.py:101
  29.3 2.0 %collective-permute-start.5 = (f16[128,2048]{1,0:T(8,128)(2,1)S(1)}, f16[128,2048]{1,0:T(8,128)(2,1)S(1)}, u32[]{:S(2)}, u32[]{:S(2)}) collective-permute-start(f16[128,2048]{1,0:T(8,128)(2,1)S(1)} %get-tuple-element.68), channel_id=1, source_target_pairs={{0,4},{4,0},{8,12},{12,8},{16,20},{20,16},{24,28},{28,24},{1,5},{5... | collective-permute-start | bytes 1572872 | tf_op jit(solution)/shard_map/ppermute | solution.py:13
  31.3 3.6 %collective-permute-done.3 = f16[128,2048]{1,0:T(8,128)(2,1)S(1)} collective-permute-done((f16[128,2048]{1,0:T(8,128)(2,1)S(1)}, f16[128,2048]{1,0:T(8,128)(2,1)S(1)}, u32[]{:S(2)}, u32[]{:S(2)}) %collective-permute-start.3) | collective-permute-done | bytes 524320 | tf_op jit(solution)/shard_map/ppermute | solution.py:13
  40.5 1.6 %collective-permute-start.16 = (bf16[2,256,512]{2,1,0:T(8,128)(2,1)S(1)}, bf16[2,256,512]{2,1,0:T(8,128)(2,1)S(1)}, u32[]{:S(2)}, u32[]{:S(2)}) collective-permute-start(bf16[2,256,512]{2,1,0:T(8,128)(2,1)S(1)} %get-tuple-element.34), channel_id=1, source_target_pairs={{0,8},{4,12},{8,0},{12,4},{16,24},{20,28},{24,16},{28,20},{1,9},{5... | collective-permute-start | bytes 1572872 | tf_op jit(solution)/shard_map/ppermute | solution.py:13
  42.1 8.4 %collective-permute-done.8 = f16[2,128,512]{2,1,0:T(8,128)(2,1)S(1)} collective-permute-done((f16[2,128,512]{2,1,0:T(8,128)(2,1)S(1)}, f16[2,128,512]{2,1,0:T(8,128)(2,1)S(1)}, u32[]{:S(2)}, u32[]{:S(2)}) %collective-permute-start.8) | collective-permute-done | bytes 262176 | tf_op jit(solution)/shard_map/ppermute | solution.py:13
  50.7 2.7 %collective-permute-start.11 = (f16[1,128,512]{2,1,0:T(8,128)(2,1)S(1)}, f16[1,128,512]{2,1,0:T(8,128)(2,1)S(1)}, u32[]{:S(2)}, u32[]{:S(2)}) collective-permute-start(f16[1,128,512]{2,1,0:T(8,128)(2,1)S(1)} %multiply_convert_fusion.14), channel_id=1, source_target_pairs={{0,16},{4,20},{8,24},{12,28},{16,0},{20,4},{24,8},{28,12},{1,17},{... | collective-permute-start | bytes 393224 | tf_op jit(solution)/shard_map/ppermute | solution.py:13
  57.3 2.9 %collective-permute-start.12 = (f16[128,2048]{1,0:T(8,128)(2,1)S(1)}, f16[128,2048]{1,0:T(8,128)(2,1)S(1)}, u32[]{:S(2)}, u32[]{:S(2)}) collective-permute-start(f16[128,2048]{1,0:T(8,128)(2,1)S(1)} %get-tuple-element.62), channel_id=1, source_target_pairs={{0,4},{4,0},{8,12},{12,8},{16,20},{20,16},{24,28},{28,24},{1,5},{5... | collective-permute-start | bytes 1572872 | tf_op jit(solution)/shard_map/ppermute | solution.py:13
  60.2 5.4 %collective-permute-done.16 = bf16[2,256,512]{2,1,0:T(8,128)(2,1)S(1)} collective-permute-done((bf16[2,256,512]{2,1,0:T(8,128)(2,1)S(1)}, bf16[2,256,512]{2,1,0:T(8,128)(2,1)S(1)}, u32[]{:S(2)}, u32[]{:S(2)}) %collective-permute-start.16) | collective-permute-done | bytes 524320 | tf_op jit(solution)/shard_map/ppermute | solution.py:13
  67.2 1.9 %collective-permute-done.12 = f16[128,2048]{1,0:T(8,128)(2,1)S(1)} collective-permute-done((f16[128,2048]{1,0:T(8,128)(2,1)S(1)}, f16[128,2048]{1,0:T(8,128)(2,1)S(1)}, u32[]{:S(2)}, u32[]{:S(2)}) %collective-permute-start.12) | collective-permute-done | bytes 524320 | tf_op jit(solution)/shard_map/ppermute | solution.py:13
  69.6 3.6 %collective-permute-start.10 = (f16[2,128,512]{2,1,0:T(8,128)(2,1)S(1)}, f16[2,128,512]{2,1,0:T(8,128)(2,1)S(1)}, u32[]{:S(2)}, u32[]{:S(2)}) collective-permute-start(f16[2,128,512]{2,1,0:T(8,128)(2,1)S(1)} %multiply_convert_fusion.5), channel_id=1, source_target_pairs={{0,8},{4,12},{8,0},{12,4},{16,24},{20,28},{24,16},{28,20},{1,9},{5... | collective-permute-start | bytes 786440 | tf_op jit(solution)/shard_map/ppermute | solution.py:13
  73.6 6.6 %collective-permute-done.10 = f16[2,128,512]{2,1,0:T(8,128)(2,1)S(1)} collective-permute-done((f16[2,128,512]{2,1,0:T(8,128)(2,1)S(1)}, f16[2,128,512]{2,1,0:T(8,128)(2,1)S(1)}, u32[]{:S(2)}, u32[]{:S(2)}) %collective-permute-start.10) | collective-permute-done | bytes 262176 | tf_op jit(solution)/shard_map/ppermute | solution.py:13
  81.6 1.6 %collective-permute-done.13 = f16[2,128,512]{2,1,0:T(8,128)(2,1)S(1)} collective-permute-done((f16[2,128,512]{2,1,0:T(8,128)(2,1)S(1)}, f16[2,128,512]{2,1,0:T(8,128)(2,1)S(1)}, u32[]{:S(2)}, u32[]{:S(2)}) %collective-permute-start.13) | collective-permute-done | bytes 262176 | tf_op jit(solution)/shard_map/ppermute | solution.py:13
  84.8 2.9 %collective-permute-done.14 = f16[1,128,512]{2,1,0:T(8,128)(2,1)S(1)} collective-permute-done((f16[1,128,512]{2,1,0:T(8,128)(2,1)S(1)}, f16[1,128,512]{2,1,0:T(8,128)(2,1)S(1)}, u32[]{:S(2)}, u32[]{:S(2)}) %collective-permute-start.14) | collective-permute-done | bytes 131104 | tf_op jit(solution)/shard_map/ppermute | solution.py:13
  87.8 3.0 %collective-permute-done.15 = f16[1,128,512]{2,1,0:T(8,128)(2,1)S(1)} collective-permute-done((f16[1,128,512]{2,1,0:T(8,128)(2,1)S(1)}, f16[1,128,512]{2,1,0:T(8,128)(2,1)S(1)}, u32[]{:S(2)}, u32[]{:S(2)}) %collective-permute-start.15) | collective-permute-done | bytes 131104 | tf_op jit(solution)/shard_map/ppermute | solution.py:13
  95.6 2.0 %collective-permute-start.22 = (f16[128,512]{1,0:T(8,128)(2,1)S(1)}, f16[128,512]{1,0:T(8,128)(2,1)S(1)}, u32[]{:S(2)}, u32[]{:S(2)}) collective-permute-start(f16[128,512]{1,0:T(8,128)(2,1)S(1)} %multiply_convert_fusion.11), channel_id=1, source_target_pairs={{0,2},{1,3},{2,0},{3,1},{4,6},{5,7},{6,4},{7,5},{8,10},{9,11},{10,... | collective-permute-start | bytes 393224 | tf_op jit(solution)/shard_map/ppermute | solution.py:13
  98.1 9.5 %collective-permute-done.21 = f16[392,512]{1,0:T(8,128)(2,1)S(1)} collective-permute-done((f16[392,512]{1,0:T(8,128)(2,1)S(1)}, f16[392,512]{1,0:T(8,128)(2,1)S(1)}, u32[]{:S(2)}, u32[]{:S(2)}) %collective-permute-start.21) | collective-permute-done | bytes 401440 | tf_op jit(solution)/shard_map/ppermute | solution.py:13
  108.2 2.3 %collective-permute-start.23 = (f16[136,512]{1,0:T(8,128)(2,1)S(1)}, f16[136,512]{1,0:T(8,128)(2,1)S(1)}, u32[]{:S(2)}, u32[]{:S(2)}) collective-permute-start(f16[136,512]{1,0:T(8,128)(2,1)S(1)} %pad_maximum_fusion.9), channel_id=1, source_target_pairs={{0,24},{4,28},{8,16},{12,20},{16,8},{20,12},{24,0},{28,4},{1,25},{... | collective-permute-start | bytes 417800 | tf_op jit(solution)/shard_map/ppermute | solution.py:13
  110.8 2.2 %collective-permute-start.25 = (f16[136,512]{1,0:T(8,128)(2,1)S(1)}, f16[136,512]{1,0:T(8,128)(2,1)S(1)}, u32[]{:S(2)}, u32[]{:S(2)}) collective-permute-start(f16[136,512]{1,0:T(8,128)(2,1)S(1)} %pad_maximum_fusion.11), channel_id=1, source_target_pairs={{0,8},{4,12},{8,0},{12,4},{16,24},{20,28},{24,16},{28,20},{1,9},{5... | collective-permute-start | bytes 417800 | tf_op jit(solution)/shard_map/ppermute | solution.py:13
  113.0 3.8 %collective-permute-done.23 = f16[136,512]{1,0:T(8,128)(2,1)S(1)} collective-permute-done((f16[136,512]{1,0:T(8,128)(2,1)S(1)}, f16[136,512]{1,0:T(8,128)(2,1)S(1)}, u32[]{:S(2)}, u32[]{:S(2)}) %collective-permute-start.23) | collective-permute-done | bytes 139296 | tf_op jit(solution)/shard_map/ppermute | solution.py:13
  116.7 4.9 %collective-permute-done.24 = f16[136,512]{1,0:T(8,128)(2,1)S(1)} collective-permute-done((f16[136,512]{1,0:T(8,128)(2,1)S(1)}, f16[136,512]{1,0:T(8,128)(2,1)S(1)}, u32[]{:S(2)}, u32[]{:S(2)}) %collective-permute-start.24) | collective-permute-done | bytes 139296 | tf_op jit(solution)/shard_map/ppermute | solution.py:13
  (142 shorter events, 30.1 us)
Async XLA Ops:
  0.0 14.5 %collective-permute-start = (bf16[256,2048]{1,0:T(8,128)(2,1)}, bf16[256,2048]{1,0:T(8,128)(2,1)S(1)}, u32[]{:S(2)}, u32[]{:S(2)}) collective-permute-start(bf16[256,2048]{1,0:T(8,128)(2,1)} %param.3), channel_id=1, source_target_pairs={{0,1},{1,0},{2,3},{3,2},{4,5},{5,4},{6,7},{7,6},{8,9},{9,8},{10,11... | collective-permute-start | bytes 3145736 | tf_op jit(solution)/shard_map/ppermute | solution.py:13
  0.5 27.2 %collective-permute-start.2 = (bf16[256,2048]{1,0:T(8,128)(2,1)}, bf16[256,2048]{1,0:T(8,128)(2,1)S(1)}, u32[]{:S(2)}, u32[]{:S(2)}) collective-permute-start(bf16[256,2048]{1,0:T(8,128)(2,1)} %param.3), channel_id=1, source_target_pairs={{0,2},{1,3},{2,0},{3,1},{4,6},{5,7},{6,4},{7,5},{8,10},{9,11},{10,... | collective-permute-start | bytes 3145736 | tf_op jit(solution)/shard_map/ppermute | solution.py:13
  8.8 16.2 %collective-permute-start.1 = (f16[128,2048]{1,0:T(8,128)(2,1)}, f16[128,2048]{1,0:T(8,128)(2,1)}, u32[]{:S(2)}, u32[]{:S(2)}) collective-permute-start(f16[128,2048]{1,0:T(8,128)(2,1)} %get-tuple-element.66), channel_id=1, source_target_pairs={{0,4},{4,0},{8,12},{12,8},{16,20},{20,16},{24,28},{28,24},{1,5},{5... | collective-permute-start | bytes 1572872 | tf_op jit(solution)/shard_map/ppermute | solution.py:13
  11.7 27.5 %collective-permute-start.7 = (bf16[1,256,1024]{2,1,0:T(8,128)(2,1)S(1)}, bf16[1,256,1024]{2,1,0:T(8,128)(2,1)}, u32[]{:S(2)}, u32[]{:S(2)}) collective-permute-start(bf16[1,256,1024]{2,1,0:T(8,128)(2,1)S(1)} %get-tuple-element.36), channel_id=1, source_target_pairs={{0,16},{4,20},{8,24},{12,28},{16,0},{20,4},{24,8},{28,12},{1,17},{... | collective-permute-start | bytes 1572872 | tf_op jit(solution)/shard_map/ppermute | solution.py:13
  19.5 15.5 %collective-permute-start.3 = (f16[128,2048]{1,0:T(8,128)(2,1)S(1)}, f16[128,2048]{1,0:T(8,128)(2,1)S(1)}, u32[]{:S(2)}, u32[]{:S(2)}) collective-permute-start(f16[128,2048]{1,0:T(8,128)(2,1)S(1)} %get-tuple-element.64), channel_id=1, source_target_pairs={{0,4},{4,0},{8,12},{12,8},{16,20},{20,16},{24,28},{28,24},{1,5},{5... | collective-permute-start | bytes 1572872 | tf_op jit(solution)/shard_map/ppermute | solution.py:13
  29.3 27.2 %collective-permute-start.5 = (f16[128,2048]{1,0:T(8,128)(2,1)S(1)}, f16[128,2048]{1,0:T(8,128)(2,1)S(1)}, u32[]{:S(2)}, u32[]{:S(2)}) collective-permute-start(f16[128,2048]{1,0:T(8,128)(2,1)S(1)} %get-tuple-element.68), channel_id=1, source_target_pairs={{0,4},{4,0},{8,12},{12,8},{16,20},{20,16},{24,28},{28,24},{1,5},{5... | collective-permute-start | bytes 1572872 | tf_op jit(solution)/shard_map/ppermute | solution.py:13
  31.3 22.0 %collective-permute-start.4 = (bf16[256,2048]{1,0:T(8,128)(2,1)S(1)}, bf16[256,2048]{1,0:T(8,128)(2,1)S(1)}, u32[]{:S(2)}, u32[]{:S(2)}) collective-permute-start(bf16[256,2048]{1,0:T(8,128)(2,1)S(1)} %collective-permute-done.2), channel_id=1, source_target_pairs={{0,1},{1,0},{2,3},{3,2},{4,5},{5,4},{6,7},{7,6},{8,9},{9,8},{10,11... | collective-permute-start | bytes 3145736 | tf_op jit(solution)/shard_map/ppermute | solution.py:13
  35.6 21.1 %collective-permute-start.6 = (f16[2,128,512]{2,1,0:T(8,128)(2,1)S(1)}, f16[2,128,512]{2,1,0:T(8,128)(2,1)S(1)}, u32[]{:S(2)}, u32[]{:S(2)}) collective-permute-start(f16[2,128,512]{2,1,0:T(8,128)(2,1)S(1)} %multiply_convert_fusion.7), channel_id=1, source_target_pairs={{0,8},{4,12},{8,0},{12,4},{16,24},{20,28},{24,16},{28,20},{1,9},{5... | collective-permute-start | bytes 786440 | tf_op jit(solution)/shard_map/ppermute | solution.py:13
  37.3 13.2 %collective-permute-start.8 = (f16[2,128,512]{2,1,0:T(8,128)(2,1)S(1)}, f16[2,128,512]{2,1,0:T(8,128)(2,1)S(1)}, u32[]{:S(2)}, u32[]{:S(2)}) collective-permute-start(f16[2,128,512]{2,1,0:T(8,128)(2,1)S(1)} %multiply_convert_fusion.6), channel_id=1, source_target_pairs={{0,8},{4,12},{8,0},{12,4},{16,24},{20,28},{24,16},{28,20},{1,9},{5... | collective-permute-start | bytes 786440 | tf_op jit(solution)/shard_map/ppermute | solution.py:13
  40.5 25.1 %collective-permute-start.16 = (bf16[2,256,512]{2,1,0:T(8,128)(2,1)S(1)}, bf16[2,256,512]{2,1,0:T(8,128)(2,1)S(1)}, u32[]{:S(2)}, u32[]{:S(2)}) collective-permute-start(bf16[2,256,512]{2,1,0:T(8,128)(2,1)S(1)} %get-tuple-element.34), channel_id=1, source_target_pairs={{0,8},{4,12},{8,0},{12,4},{16,24},{20,28},{24,16},{28,20},{1,9},{5... | collective-permute-start | bytes 1572872 | tf_op jit(solution)/shard_map/ppermute | solution.py:13
  50.7 30.8 %collective-permute-start.11 = (f16[1,128,512]{2,1,0:T(8,128)(2,1)S(1)}, f16[1,128,512]{2,1,0:T(8,128)(2,1)S(1)}, u32[]{:S(2)}, u32[]{:S(2)}) collective-permute-start(f16[1,128,512]{2,1,0:T(8,128)(2,1)S(1)} %multiply_convert_fusion.14), channel_id=1, source_target_pairs={{0,16},{4,20},{8,24},{12,28},{16,0},{20,4},{24,8},{28,12},{1,17},{... | collective-permute-start | bytes 393224 | tf_op jit(solution)/shard_map/ppermute | solution.py:13
  56.9 16.4 %collective-permute-start.9 = (f16[1,128,512]{2,1,0:T(8,128)(2,1)S(1)}, f16[1,128,512]{2,1,0:T(8,128)(2,1)S(1)}, u32[]{:S(2)}, u32[]{:S(2)}) collective-permute-start(f16[1,128,512]{2,1,0:T(8,128)(2,1)S(1)} %multiply_convert_fusion.15), channel_id=1, source_target_pairs={{0,16},{4,20},{8,24},{12,28},{16,0},{20,4},{24,8},{28,12},{1,17},{... | collective-permute-start | bytes 393224 | tf_op jit(solution)/shard_map/ppermute | solution.py:13
  57.3 11.8 %collective-permute-start.12 = (f16[128,2048]{1,0:T(8,128)(2,1)S(1)}, f16[128,2048]{1,0:T(8,128)(2,1)S(1)}, u32[]{:S(2)}, u32[]{:S(2)}) collective-permute-start(f16[128,2048]{1,0:T(8,128)(2,1)S(1)} %get-tuple-element.62), channel_id=1, source_target_pairs={{0,4},{4,0},{8,12},{12,8},{16,20},{20,16},{24,28},{28,24},{1,5},{5... | collective-permute-start | bytes 1572872 | tf_op jit(solution)/shard_map/ppermute | solution.py:13
  65.7 25.4 %collective-permute-start.17 = (bf16[4,256,512]{2,1,0:T(8,128)(2,1)S(1)}, bf16[4,256,512]{2,1,0:T(8,128)(2,1)S(1)}, u32[]{:S(2)}, u32[]{:S(2)}) collective-permute-start(bf16[4,256,512]{2,1,0:T(8,128)(2,1)S(1)} %pad_maximum_fusion), channel_id=1, source_target_pairs={{0,4},{4,0},{8,12},{12,8},{16,20},{20,16},{24,28},{28,24},{1,5},{5... | collective-permute-start | bytes 3145736 | tf_op jit(solution)/shard_map/ppermute | solution.py:13
  69.6 10.6 %collective-permute-start.10 = (f16[2,128,512]{2,1,0:T(8,128)(2,1)S(1)}, f16[2,128,512]{2,1,0:T(8,128)(2,1)S(1)}, u32[]{:S(2)}, u32[]{:S(2)}) collective-permute-start(f16[2,128,512]{2,1,0:T(8,128)(2,1)S(1)} %multiply_convert_fusion.5), channel_id=1, source_target_pairs={{0,8},{4,12},{8,0},{12,4},{16,24},{20,28},{24,16},{28,20},{1,9},{5... | collective-permute-start | bytes 786440 | tf_op jit(solution)/shard_map/ppermute | solution.py:13
  73.5 9.8 %collective-permute-start.13 = (f16[2,128,512]{2,1,0:T(8,128)(2,1)S(1)}, f16[2,128,512]{2,1,0:T(8,128)(2,1)S(1)}, u32[]{:S(2)}, u32[]{:S(2)}) collective-permute-start(f16[2,128,512]{2,1,0:T(8,128)(2,1)S(1)} %multiply_convert_fusion.4), channel_id=1, source_target_pairs={{0,8},{4,12},{8,0},{12,4},{16,24},{20,28},{24,16},{28,20},{1,9},{5... | collective-permute-start | bytes 786440 | tf_op jit(solution)/shard_map/ppermute | solution.py:13
  80.4 7.3 %collective-permute-start.14 = (f16[1,128,512]{2,1,0:T(8,128)(2,1)S(1)}, f16[1,128,512]{2,1,0:T(8,128)(2,1)S(1)}, u32[]{:S(2)}, u32[]{:S(2)}) collective-permute-start(f16[1,128,512]{2,1,0:T(8,128)(2,1)S(1)} %multiply_convert_fusion.13), channel_id=1, source_target_pairs={{0,16},{4,20},{8,24},{12,28},{16,0},{20,4},{24,8},{28,12},{1,17},{... | collective-permute-start | bytes 393224 | tf_op jit(solution)/shard_map/ppermute | solution.py:13
  83.4 7.3 %collective-permute-start.15 = (f16[1,128,512]{2,1,0:T(8,128)(2,1)S(1)}, f16[1,128,512]{2,1,0:T(8,128)(2,1)S(1)}, u32[]{:S(2)}, u32[]{:S(2)}) collective-permute-start(f16[1,128,512]{2,1,0:T(8,128)(2,1)S(1)} %multiply_convert_fusion.12), channel_id=1, source_target_pairs={{0,16},{4,20},{8,24},{12,28},{16,0},{20,4},{24,8},{28,12},{1,17},{... | collective-permute-start | bytes 393224 | tf_op jit(solution)/shard_map/ppermute | solution.py:13
  93.2 4.4 %collective-permute-start.18 = (f32[4,128,512]{2,1,0:T(8,128)S(1)}, f32[4,128,512]{2,1,0:T(8,128)S(1)}, u32[]{:S(2)}, u32[]{:S(2)}) collective-permute-start(f32[4,128,512]{2,1,0:T(8,128)S(1)} %convolution_add_fusion.1), channel_id=1, source_target_pairs={{0,1},{1,0},{2,3},{3,2},{4,5},{5,4},{6,7},{7,6},{8,9},{9,8},{10,11... | collective-permute-start | bytes 3145736 | tf_op jit(solution)/shard_map/ppermute | solution.py:13
  95.4 12.2 %collective-permute-start.21 = (f16[392,512]{1,0:T(8,128)(2,1)S(1)}, f16[392,512]{1,0:T(8,128)(2,1)S(1)}, u32[]{:S(2)}, u32[]{:S(2)}) collective-permute-start(f16[392,512]{1,0:T(8,128)(2,1)S(1)} %pad_maximum_fusion.8), channel_id=1, source_target_pairs={{0,2},{1,3},{2,0},{3,1},{4,6},{5,7},{6,4},{7,5},{8,10},{9,11},{10,... | collective-permute-start | bytes 1204232 | tf_op jit(solution)/shard_map/ppermute | solution.py:13
  95.6 26.1 %collective-permute-start.22 = (f16[128,512]{1,0:T(8,128)(2,1)S(1)}, f16[128,512]{1,0:T(8,128)(2,1)S(1)}, u32[]{:S(2)}, u32[]{:S(2)}) collective-permute-start(f16[128,512]{1,0:T(8,128)(2,1)S(1)} %multiply_convert_fusion.11), channel_id=1, source_target_pairs={{0,2},{1,3},{2,0},{3,1},{4,6},{5,7},{6,4},{7,5},{8,10},{9,11},{10,... | collective-permute-start | bytes 393224 | tf_op jit(solution)/shard_map/ppermute | solution.py:13
  108.2 8.5 %collective-permute-start.23 = (f16[136,512]{1,0:T(8,128)(2,1)S(1)}, f16[136,512]{1,0:T(8,128)(2,1)S(1)}, u32[]{:S(2)}, u32[]{:S(2)}) collective-permute-start(f16[136,512]{1,0:T(8,128)(2,1)S(1)} %pad_maximum_fusion.9), channel_id=1, source_target_pairs={{0,24},{4,28},{8,16},{12,20},{16,8},{20,12},{24,0},{28,4},{1,25},{... | collective-permute-start | bytes 417800 | tf_op jit(solution)/shard_map/ppermute | solution.py:13
  110.6 11.0 %collective-permute-start.24 = (f16[136,512]{1,0:T(8,128)(2,1)S(1)}, f16[136,512]{1,0:T(8,128)(2,1)S(1)}, u32[]{:S(2)}, u32[]{:S(2)}) collective-permute-start(f16[136,512]{1,0:T(8,128)(2,1)S(1)} %pad_maximum_fusion.10), channel_id=1, source_target_pairs={{0,16},{4,20},{8,24},{12,28},{16,0},{20,4},{24,8},{28,12},{1,17},{... | collective-permute-start | bytes 417800 | tf_op jit(solution)/shard_map/ppermute | solution.py:13
  110.8 10.9 %collective-permute-start.25 = (f16[136,512]{1,0:T(8,128)(2,1)S(1)}, f16[136,512]{1,0:T(8,128)(2,1)S(1)}, u32[]{:S(2)}, u32[]{:S(2)}) collective-permute-start(f16[136,512]{1,0:T(8,128)(2,1)S(1)} %pad_maximum_fusion.11), channel_id=1, source_target_pairs={{0,8},{4,12},{8,0},{12,4},{16,24},{20,28},{24,16},{28,20},{1,9},{5... | collective-permute-start | bytes 417800 | tf_op jit(solution)/shard_map/ppermute | solution.py:13
  (5 other events, 24.4 us)
